TPU v7x, 256 devices: a whole 4x4x8 slice. The times are simulated.
256 devices in a mesh: ctx: 2 (over core), head: 4 (over x), sess: 32 (over z, y).
Axes of the slice: x: 4, y: 4, z: 8, core: 2. Of those that a mesh axis runs over, the one named last changes fastest.
Arguments:
- queries: bfloat16 [32, 512, 16, 128], P('sess', 'ctx', 'head'), may hold values from -6 to 6
- keys: bfloat16 [32, 512, 16, 128], P('sess', 'ctx', 'head'), may hold values from -6 to 6
- values: bfloat16 [32, 512, 32, 128], P('sess', 'ctx', 'head'), may hold values from -6 to 6
- gate_logit: float32 [32, 32, 512], P('sess', 'head', 'ctx'), may hold values from -10.1 to 0
- beta_logit: float32 [32, 32, 512], P('sess', 'head', 'ctx'), may hold values from -6 to 6
- token_blocks: int32 [32], P('sess'), may hold values from 1 to 4, as said below
- slot_map: int32 [32], replicated, may hold values from 0 to 31, as said below
Outputs:
- token_out: bfloat16 [32, 512, 32, 128], P('sess', 'ctx', 'head')
- slot_states: float32 [32, 32, 128, 128], P('sess', 'head', 'ctx')
Inputs may be any that keep to these rules, and one draw needn't show every extreme that they name: `token_blocks`: one session reaches the largest length in every draw. slot_map is a permutation of the slots; slot j belongs to index j // 1 of sess.
All inputs are finite; a program needn't handle non-finite values.
Results may differ from a plain program's by a relative error of at most 0.0011.
Values sent between devices are 32-bit elements; how exact they have to be, the bound alone decides.
No kernel may reach another device: no remote copies, remote signals or barrier semaphores. Data moves between devices by JAX's collectives and lax.ppermute only.
A program may use at most 64 MiB of HBM per device.

v0:
```python
import jax
import jax.numpy as jnp
from jax import lax
from jax.sharding import PartitionSpec as P

QK_HEADS = 16
VALUE_HEADS = 32
SPAN = 128
BLOCK = 128


HIGH_PRECISION = lax.Precision.HIGHEST


def entering(part, axis, combine, identity):
    place = lax.axis_index(axis)
    gathered = jax.tree.map(lambda a: lax.all_gather(a, axis), part)
    state = jax.tree.map(lambda a, e: jnp.zeros_like(a) + jnp.asarray(e, a.dtype), part, identity)

    def one(step, state):
        return combine(
            state, jax.tree.map(lambda a: lax.dynamic_index_in_dim(a, step, 0, False), gathered)
        )

    return lax.fori_loop(0, place, one, state)


def spread_2(x, axis, root):
    mine = lax.axis_index(axis) == root
    return lax.psum(jnp.where(mine, x, jnp.zeros_like(x)), axis)


def unit_rows(x):
    x = x.astype(jnp.float32)
    return x * lax.rsqrt(jnp.sum(x * x, axis=-1, keepdims=True) + 1e-06)


def compose(earlier, later):
    first_map, first_state = earlier
    second_map, second_state = later
    joined_map = jnp.einsum("bij,bjk->bik", second_map, first_map, precision=HIGH_PRECISION)
    joined_state = (
        jnp.einsum("bij,bjv->biv", second_map, first_state, precision=HIGH_PRECISION) + second_state
    )
    return (joined_map, joined_state)


def local(queries, keys, values, gate_logit, beta_logit, token_blocks, slot_map):
    sess_loc, tok_loc, qk_loc, dk = queries.shape
    head_loc = values.shape[2]
    dv = values.shape[3]
    group = VALUE_HEADS // QK_HEADS
    batch = sess_loc * head_loc
    blocks = tok_loc // SPAN
    nctx = lax.axis_size("ctx")
    ctx_at = lax.axis_index("ctx")

    def arrange(x):
        return x.transpose(0, 2, 1, 3).reshape(batch, blocks, SPAN, x.shape[3])

    qn = arrange(jnp.repeat(unit_rows(queries), group, axis=2))
    kn = arrange(jnp.repeat(unit_rows(keys), group, axis=2))
    vf = arrange(values.astype(jnp.float32))
    slot_places = ctx_at * tok_loc + jnp.arange(tok_loc, dtype=jnp.int32)
    live = slot_places[None, :] < (token_blocks * BLOCK)[:, None]
    live_heads = jnp.broadcast_to(live[:, None, :], (sess_loc, head_loc, tok_loc))
    log_decay = jnp.where(live_heads, -jax.nn.softplus(gate_logit), 0.0).reshape(
        batch, blocks, SPAN
    )
    beta = jnp.where(live_heads, jax.nn.sigmoid(beta_logit), 0.0).reshape(batch, blocks, SPAN)
    running = jnp.cumsum(log_decay, axis=-1)
    gamma = jnp.exp(running)
    spread = running[..., :, None] - running[..., None, :]
    rows_at = jnp.arange(SPAN)[:, None]
    cols_at = jnp.arange(SPAN)[None, :]
    decay_pair = jnp.where(rows_at >= cols_at, jnp.exp(jnp.minimum(spread, 0.0)), 0.0)
    key_key = jnp.einsum("bnck,bnek->bnce", kn, kn, precision=HIGH_PRECISION)
    lower = jnp.where(rows_at > cols_at, beta[..., :, None] * decay_pair * key_key, 0.0)
    unit = jnp.eye(SPAN, dtype=jnp.float32)
    inverse = lax.linalg.triangular_solve(
        unit + lower,
        jnp.broadcast_to(unit, lower.shape),
        left_side=True,
        lower=True,
        unit_diagonal=True,
    )
    writes = jnp.einsum("bnce,bned->bncd", inverse, beta[..., None] * vf, precision=HIGH_PRECISION)
    erase = jnp.einsum(
        "bnce,bnek->bnck", inverse, (beta * gamma)[..., None] * kn, precision=HIGH_PRECISION
    )
    tail = running[..., -1:]
    keys_end = jnp.exp(tail - running)[..., None] * kn
    gamma_end = jnp.exp(tail[..., 0])
    query_key = decay_pair * jnp.einsum("bnck,bnek->bnce", qn, kn, precision=HIGH_PRECISION)

    def by_block(x):
        return jnp.moveaxis(x, 1, 0)

    eye_key = jnp.eye(dk, dtype=jnp.float32)
    start_map = jnp.broadcast_to(eye_key, (batch, dk, dk))
    start_state = jnp.zeros((batch, dk, dv), jnp.float32)

    def map_step(carry, items):
        acc_map, acc_state = carry
        end_decay, expanded_keys, erase_b, batched_writes = items
        block_map = end_decay[:, None, None] * eye_key - jnp.einsum(
            "bck,bcj->bkj", expanded_keys, erase_b, precision=HIGH_PRECISION
        )
        acc_state = jnp.einsum(
            "bij,bjv->biv", block_map, acc_state, precision=HIGH_PRECISION
        ) + jnp.einsum("psh,psf->phf", expanded_keys, batched_writes, precision=HIGH_PRECISION)
        acc_map = jnp.einsum("bij,bjk->bik", block_map, acc_map, precision=HIGH_PRECISION)
        return ((acc_map, acc_state), None)

    (made_map, made_state), unused = lax.scan(
        map_step,
        (start_map, start_state),
        (by_block(gamma_end), by_block(keys_end), by_block(erase), by_block(writes)),
    )
    prefix = entering((made_map, made_state), "ctx", compose, (start_map, start_state))
    incoming = prefix[1]

    def read_step(recurrent_state, items):
        gam, end_decay, expanded_keys, erase_b, batched_writes, query_b, pair_b = items
        delta = batched_writes - jnp.einsum(
            "bck,bkv->bcv", erase_b, recurrent_state, precision=HIGH_PRECISION
        )
        final_result = gam[..., None] * jnp.einsum(
            "bck,bkv->bcv", query_b, recurrent_state, precision=HIGH_PRECISION
        ) + jnp.einsum("bce,bev->bcv", pair_b, delta, precision=HIGH_PRECISION)
        recurrent_state = end_decay[:, None, None] * recurrent_state + jnp.einsum(
            "bck,bcv->bkv", expanded_keys, delta, precision=HIGH_PRECISION
        )
        return (recurrent_state, final_result)

    end_state, results = lax.scan(
        read_step,
        incoming,
        (
            by_block(gamma),
            by_block(gamma_end),
            by_block(keys_end),
            by_block(erase),
            by_block(writes),
            by_block(qn),
            by_block(query_key),
        ),
    )
    results = (
        jnp.moveaxis(results, 0, 1).reshape(sess_loc, head_loc, tok_loc, dv).transpose(0, 2, 1, 3)
    )
    token_out = jnp.where(live[:, :, None, None], results, 0.0).astype(jnp.bfloat16)
    final_state = spread_2(end_state, "ctx", nctx - 1)
    row_count = dk // nctx
    final_rows = lax.dynamic_slice_in_dim(
        final_state.reshape(sess_loc, head_loc, dk, dv), ctx_at * row_count, row_count, 2
    )
    sess_at = lax.axis_index("sess")
    mine = sess_at * sess_loc + jnp.arange(sess_loc, dtype=jnp.int32)
    match = slot_map[None, :] == mine[:, None]
    collected = lax.all_gather(final_rows, "sess", axis=0, tiled=True)
    pick = match.astype(jnp.float32)
    slot_states = jnp.einsum("ln,nhrd->lhrd", pick, collected, precision=HIGH_PRECISION)
    return (token_out, slot_states)


def solution(mesh):
    placed = (
        P("sess", "ctx", "head", None),
        P("sess", "ctx", "head", None),
        P("sess", "ctx", "head", None),
        P("sess", "head", "ctx"),
        P("sess", "head", "ctx"),
        P("sess"),
        P(),
    )
    return jax.shard_map(
        local,
        mesh=mesh,
        in_specs=placed,
        out_specs=(P("sess", "ctx", "head", None), P("sess", "head", "ctx", None)),
        check_vma=False,
    )
```

profile of v0, /device:TPU:6, one launch (start us, length us, event | category | flops | bytes accessed | tf_op | source)
XLA Modules:
  0.0 396.7 jit_solution(1528268349759713922)
XLA Ops:
  7.2 0.0 all-gather.7.cloned.1.call-start
  7.9 0.7 fusion.61
  8.6 0.6 reduce_window_sum.13
  9.2 0.2 slice_reduce_fusion
  9.4 0.1 iota_compare_fusion.4
  9.5 1.3 fusion.50
  10.9 1.3 fusion.51
  12.2 0.8 exponential_multiply_fusion
  13.0 0.1 broadcast_in_dim.74
  13.1 0.3 multiply_bitcast_fusion
  13.4 0.3 copy.57
  13.8 3.4 fusion.44
  17.1 158.0 %custom-call.3 = f32[8,2,1,128,128]{3,4,2,1,0:T(8,128)S(1)} custom-call(f32[8,2,1,128,128]{4,3,2,1,0:T(8,128)} %fusion.44), custom_call_target="InvertDiagBlocksLowerTriangular" | custom-call | tf_op jit(solution)/shard_map/triangular_solve | solution.py:80
  175.1 1.8 fusion.46
  177.0 0.0 copy-done.2
  177.0 1.2 convolution_bitcast_fusion.2
  178.2 0.1 copy.58
  178.3 1.1 convert_bitcast_fusion
  179.4 0.2 copy.56
  179.7 1.2 convolution_bitcast_fusion.1
  180.9 1.1 copy.59
  182.0 0.0 copy-start.3
  182.0 10.3 %while.39 = (s32[]{:T(128)}, f32[8,128,128]{2,1,0:T(8,128)S(1)}, f32[8,128,128]{2,1,0:T(8,128)}, f32[2,8]{1,0:T(2,128)S(1)}, f32[2,8,128,128]{2,3,1,0:T(8,128)S(...) while((s32[]{:T(128)}, f32[8,128,128]{2,1,0:T(8,128)S(1)}, ...), condition=%wide.region_3.4_spmd.clone, body=%wide.region_2.3_spmd.clone.sunk | while | flops 805863424 | bytes 7998131 | solution.py:115
  182.2 0.6 convolution_subtract_fusion.5
  182.9 0.7 fusion.126
  183.6 0.7 fusion.127
  184.3 2.5 convolution_add_fusion.9
  186.8 0.6 convolution_subtract_fusion.5
  187.5 0.7 fusion.126
  188.2 1.7 fusion.127
  189.8 2.5 convolution_add_fusion.9
  192.3 0.8 copy-done
  193.1 0.0 all-gather.7.cloned.1.call-update
  193.2 0.0 all-gather.9.cloned.1.call-start
  193.2 0.7 all-gather.9.cloned.1.call-update
  193.9 0.0 all-reduce.2.cloned.1.call-start
  194.0 0.3 fusion.52
  194.4 0.3 fusion.53
  194.8 0.1 broadcast_in_dim.79
  194.9 0.0 copy-start.1
  194.9 1.0 copy-done.1
  195.9 4.5 %fusion.39 = f32[2,8,128,128]{3,2,0,1:T(8,128)} fusion(f32[8,2,128,128]{3,2,1,0:T(8,128)S(1)} %bitcast.165, f32[8,2,128,128]{3,2,1,0:T(8,128)} %bitcast.170, f32[2,8,128]{2,0,1:T(2,128)S(1)} %copy.61, pred[128,128]{1,0:T(8,128)(4,1)S(1)} %get-tuple-element.271), kind=kOutput, calls=%fused_computation.50 | convolution fusion | flops 403701760 | bytes 3170304 | tf_op jit(solution)/shard_map/bnck,bnek->bnce/dot_general | solution.py:94
  200.4 10.2 %all-gather.7.cloned.1.call-done = f32[16,128,128]{2,1,0:T(8,128)} async-done(((f32[8,128,128]{2,1,0:T(8,128)}), f32[16,128,128]{2,1,0:T(8,128)}) %all-gather.7.cloned.1.call-update) | async-done | bytes 1048592 | tf_op jit(solution)/shard_map/all_gather | solution.py:17
  210.6 18.1 %all-gather.9.cloned.1.call-done = f32[16,128,128]{2,1,0:T(8,128)} async-done(((f32[8,128,128]{2,1,0:T(8,128)}), f32[16,128,128]{2,1,0:T(8,128)}) %all-gather.9.cloned.1.call-update) | async-done | bytes 1048592 | tf_op jit(solution)/shard_map/all_gather | solution.py:17
  228.7 0.0 copy-start.4
  228.7 13.4 %while.38 = (s32[]{:T(128)}, f32[8,128,128]{2,1,0:T(8,128)S(1)}, bf16[2,8,128,128]{3,2,1,0:T(8,128)(2,1)}, f32[2,8]{1,0:T(2,128)S(1)}, f32[2,8,128,128]{2,3,1,0:...) while((s32[]{:T(128)}, f32[8,128,128]{2,1,0:T(8,128)S(1)}, ...), condition=%wide.region_8.9_spmd, body=%wide.region_7.8_spmd.sunk | while | flops 805961728 | bytes 7879365 | solution.py:136
  228.7 1.7 convolution_multiply_fusion.3
  230.5 1.7 convolution_subtract_fusion.4
  232.2 0.8 convolution_add_fusion.8
  233.0 2.4 fusion.115
  235.4 1.7 convolution_multiply_fusion.3
  237.2 1.7 convolution_subtract_fusion.4
  238.9 0.8 convolution_add_fusion.8
  239.7 2.4 fusion.115
  242.1 0.8 broadcast_select_fusion
  243.0 0.0 all-reduce.2.cloned.1.call-update
  243.0 0.3 all-gather.11.cloned.1.call-start
  243.3 32.6 %all-reduce.2.cloned.1.call-done = f32[8,128,128]{2,1,0:T(8,128)} async-done(((f32[8,128,128]{2,1,0:T(8,128)}), f32[8,128,128]{2,1,0:T(8,128)}) %all-reduce.2.cloned.1.call-update) | async-done | bytes 524304 | tf_op jit(solution)/shard_map/psum | solution.py:30
  275.8 1.7 constant_dynamic-slice_fusion.2
  277.5 0.0 all-gather.11.cloned.1.call-update
  277.5 1.4 copy.69
  278.9 1.1 fusion.45
  280.0 99.0 %all-gather.11.cloned.1.call-done = f32[256,64,128]{2,1,0:T(8,128)} async-done(((f32[8,64,128]{2,1,0:T(8,128)}), f32[256,64,128]{2,1,0:T(8,128)}) %all-gather.11.cloned.1.call-update) | async-done | bytes 8388624 | tf_op jit(solution)/shard_map/all_gather | solution.py:161
  379.0 11.1 %fusion.37 = f32[1,8,64,128]{3,0,2,1:T(1,128)} fusion(f32[32,8,64,128]{3,2,1,0:T(8,128)} %bitcast.171, s32[32]{0:T(128)S(1)} %copy-done.4, s32[]{:T(128)S(6)} %axis_index.33), kind=kOutput, calls=%fused_computation.47 | convolution fusion | flops 25165856 | bytes 8650884 | tf_op jit(solution)/shard_map/ln,nhrd->lhrd/dot_general | solution.py:163
  (34 shorter events, 0.4 us)
Async XLA Ops:
  7.2 203.4 %all-gather.7.cloned.1.call-start = ((), (), s32[]{:S(2)}) async-start(), calls=%async_computation.1 | async-start | bytes 1572864 | tf_op jit(solution)/shard_map/all_gather | solution.py:17
  13.1 163.9 %copy-start.2 = (f32[256,4,2,128]{3,0,2,1:T(8,128)}, f32[256,4,2,128]{3,0,2,1:T(8,128)S(1)}, u32[]{:S(2)}) copy-start(f32[256,4,2,128]{3,0,2,1:T(8,128)S(1)} %broadcast_in_dim.74) | copy-start | bytes 3145732
  182.0 12.0 %copy-start.3 = (bf16[1,256,4,128]{3,2,1,0:T(4,128)(2,1)S(1)}, bf16[1,256,4,128]{3,2,1,0:T(4,128)(2,1)}, u32[]{:S(2)}) copy-start(bf16[1,256,4,128]{3,2,1,0:T(4,128)(2,1)} %param.13) | copy-start | bytes 786436
  192.3 0.8 copy-start
  193.2 35.5 %all-gather.9.cloned.1.call-start = ((), (), s32[]{:S(2)}) async-start(), calls=%async_computation.2 | async-start | bytes 1572864 | tf_op jit(solution)/shard_map/all_gather | solution.py:17
  193.9 81.9 %all-reduce.2.cloned.1.call-start = ((), (), s32[]{:S(2)}) async-start(), calls=%async_computation | async-start | bytes 1048576 | tf_op jit(solution)/shard_map/psum | solution.py:30
  194.9 1.0 copy-start.1
  228.7 150.3 %copy-start.4 = (s32[32]{0:T(128)S(1)}, s32[32]{0:T(128)}, u32[]{:S(2)}) copy-start(s32[32]{0:T(128)} %param.19) | copy-start | bytes 388
  243.0 136.1 %all-gather.11.cloned.1.call-start = ((), (), s32[]{:S(2)}) async-start(), calls=%async_computation.3 | async-start | bytes 8650752 | tf_op jit(solution)/shard_map/all_gather | solution.py:161
Sparse Core Ops, SparseCore 0:
  193.3 17.2 all-gather.6
  213.0 15.6 all-gather.8
  243.1 32.6 all-reduce.1
  279.2 99.8 all-gather.10
where the time goes:
time: 398 us; the launch traced here: 397 us
  other arithmetic  167 us (42%)
  waiting for transfers between devices  161 us (40%)
  matrix products  46.5 us (12%)
  between operations  14.7 us (4%)
  local copies, waits for them, and re-layouts  7.18 us (2%)
    another operation x4, other arithmetic, local(): lax.linalg.triangular_solve(unit + lower, jnp.broadcast_to(unit, lower.sh...  158 us
    all_gather x1, waiting for transfers between devices, local(): collected = lax.all_gather(final_rows, 'sess', axis=0, tiled=True)  99 us
    psum x1, waiting for transfers between devices, spread_2(): return lax.psum(jnp.where(mine, x, jnp.zeros_like(x)), axis)  32.6 us
    all_gather x2, waiting for transfers between devices, entering(): gathered = jax.tree.map(lambda a: lax.all_gather(a, axis), part)  28.2 us
    dot_general x1, matrix products, local(): jnp.einsum('ln,nhrd->lhrd', pick, collected, precision=HIGH_PRECISION)  11.1 us
  transfers between devices with their start and end apart: 4, of which 4 were waited for; matrix products, arithmetic and copies ran while one was open for 2% of the time, Pallas kernels for 0%

commit v1 on v0

v1 whole, which is shorter than its diff:
```python
import functools
import jax
import jax.numpy as jnp
from jax import lax
from jax.experimental import pallas as pl
from jax.experimental.pallas import tpu as pltpu

F32 = jnp.float32
BF16 = jnp.bfloat16


def split(x):
    hi = x.astype(BF16)
    return hi, (x - hi.astype(F32)).astype(BF16)


def mm(a, b):
    return jnp.dot(a, b, preferred_element_type=F32)


def mm_nt(a, b):
    return lax.dot_general(a, b, (((1,), (1,)), ((), ())), preferred_element_type=F32)


def pack_left(a):
    hi, lo = split(a)
    return jnp.concatenate([hi, lo], axis=1)


def pack_right(b):
    hi, lo = split(b)
    row = jnp.concatenate([hi, lo], axis=1)
    return jnp.concatenate([row, row], axis=0)


def fold(r):
    return r[:, :128] + r[:, 128:]


def mm_small(a, b):
    return fold(mm(pack_left(a), pack_right(b)))


def mm_wide(a, b):
    ah, al = split(a)
    bh, bl = split(b)
    return mm(jnp.concatenate([ah, al], axis=1), jnp.concatenate([bh, bh], axis=0)) + mm(ah, bl)


def decay_rows(gate, live):
    x = jnp.where(live, -(jnp.maximum(gate, 0.0) + jnp.log1p(jnp.exp(-jnp.abs(gate)))), 0.0)
    lane = lax.broadcasted_iota(jnp.int32, x.shape, 1)
    step = 1
    while step < 256:
        x = x + jnp.where(lane >= step, pltpu.roll(x, step, 1), 0.0)
        step *= 2
    return x


def to_columns(rows):
    pad = jnp.zeros((128 - rows.shape[0], 256), F32)
    return jnp.concatenate([rows, pad], axis=0).T


def live_lanes(info_ref):
    edge = info_ref[1] * 128 - info_ref[0] * 256
    return lax.broadcasted_iota(jnp.int32, (8, 256), 1) < edge


def log_norm(x):
    return -0.5 * jnp.log(jnp.sum(x * x, axis=1, keepdims=True) + 1e-06)


def maps_kernel(
    info_ref, k_ref, v_ref, g_ref, b_ref, pay_ref, keep_ref, y_ref,
    kf, vf, acol, rcol, bcol, zcol, brow, gend, l11, l21, l22, cmp_ref, xc,
):
    kf[...] = k_ref[...].astype(F32)
    vf[...] = v_ref[...].astype(F32)
    live = live_lanes(info_ref)
    G = decay_rows(g_ref[...], live)
    logit = b_ref[...]
    beta = jnp.where(live, 1.0 / (1.0 + jnp.exp(-logit)), 0.0)
    cols = to_columns(jnp.concatenate([G, beta], axis=0))
    lane = lax.broadcasted_iota(jnp.int32, (256, 128), 1)
    norms = jnp.zeros((256, 128), F32)
    for kh in range(4):
        x = kf[pl.ds(kh, 256, stride=4), :]
        norms = jnp.where(lane == kh, log_norm(x), norms)
    norm_rows = norms.T
    for h in range(8):
        kh = h // 2
        g_c = cols[:, h : h + 1]
        be_c = cols[:, 8 + h : 9 + h]
        n_c = norms[:, kh : kh + 1]
        a = g_c + jnp.log(be_c) + n_c
        acol[h] = jnp.broadcast_to(a, (256, 128))
        rcol[h] = jnp.broadcast_to(jnp.exp(a), (256, 128))
        bcol[h] = jnp.broadcast_to(be_c, (256, 128))
        last = G[h : h + 1, 255:256]
        zcol[h] = jnp.broadcast_to(jnp.exp(last - g_c + n_c), (256, 128))
        brow[h] = jnp.broadcast_to(G[h : h + 1, :] - norm_rows[kh : kh + 1, :], (8, 256))
        gend[h] = jnp.broadcast_to(jnp.exp(last), (8, 128))

    row = lax.broadcasted_iota(jnp.int32, (128, 128), 0)
    col = lax.broadcasted_iota(jnp.int32, (128, 128), 1)
    lower = row > col

    def build(kh, c):
        k = kf[pl.ds(kh, 256, stride=4), :].astype(BF16)
        k1, k2 = k[:128], k[128:]
        kk1 = mm_nt(k1, k1)
        kk2 = mm_nt(k2, k)
        for s in range(2):
            h = 2 * kh + s
            a1, a2 = acol[h, :128], acol[h, 128:]
            b1, b2 = brow[h, 0:1, :128], brow[h, 0:1, 128:]
            l11[h] = jnp.where(lower, jnp.exp(a1 - b1) * kk1, 0.0)
            l21[h] = jnp.exp(a2 - b1) * kk2[:, :128]
            l22[h] = jnp.where(lower, jnp.exp(a2 - b2) * kk2[:, 128:], 0.0)
        return c

    lax.fori_loop(0, 4, build, 0)

    group = lax.broadcasted_iota(jnp.int32, (32, 128), 1) // 32
    for half in range(2):
        for kb in range(8):
            src = l11 if kb < 4 else l22
            r0 = (kb % 4) * 32
            acc = jnp.zeros((32, 128), F32)
            for q in range(4):
                t = src[half * 4 + q, r0 : r0 + 32, :]
                shift = (q * 32 - r0) % 128
                if shift:
                    t = pltpu.roll(t, shift, 1)
                acc = jnp.where(group == q, t, acc)
            cmp_ref[half, kb * 32 : kb * 32 + 32, :] = acc

    lane8 = lax.broadcasted_iota(jnp.int32, (8, 128), 1)
    base = (lane8 // 32) * 32
    inner = lane8 % 32
    for half in range(2):
        xs = []
        for i in range(32):
            acc = jnp.where(inner == i, 1.0, 0.0).astype(F32)
            if i:
                r = cmp_ref[half, pl.ds(i, 8, stride=32), :]
                for j in range(i):
                    coef = jnp.take_along_axis(r, base + j, axis=1, mode="promise_in_bounds")
                    acc = acc - coef * xs[j]
            xs.append(acc)
            xc[half, pl.ds(i, 8, stride=32), :] = acc

    block = row // 32 == col // 32
    odd64 = (row // 64 == col // 64) & (row // 32 != col // 32) & lower
    odd128 = (row // 64 != col // 64) & lower
    eye = row == col

    def solve(it, c):
        for s in range(HEADS_PER_STEP):
            h = it * HEADS_PER_STEP + s
            kh = h // 2
            idx = (h % 4) * 32 + col % 32
            inv = []
            for part, src in ((0, l11), (1, l22)):
                x = xc[h // 4, part * 128 : part * 128 + 128, :]
                x = jnp.take_along_axis(x, idx, axis=1, mode="promise_in_bounds")
                x = jnp.where(block, x, 0.0)
                l = src[h]
                for mask in (odd64, odd128):
                    m = mm_small(jnp.where(mask, l, 0.0), x)
                    x = x - mm_small(x, m)
                inv.append(x)
            k = kf[pl.ds(kh, 256, stride=4), :]
            v = vf[pl.ds(h, 256, stride=8), :]
            r = jnp.concatenate([rcol[h] * k, bcol[h] * v], axis=1)
            y1 = mm_wide(inv[0], r[:128])
            y2 = mm_wide(inv[1], r[128:] - mm_wide(l21[h], y1))
            y_ref[h, :128] = y1
            y_ref[h, 128:] = y2
            z = zcol[h]
            zz = jnp.concatenate([z, z], axis=1)
            zh, zl = split(zz * jnp.concatenate([y1, y2], axis=0))
            kt = k.astype(BF16).T
            st = mm(kt, zh) + mm(kt, zl)
            t = jnp.where(eye, gend[h, 0:1, :], 0.0) - st[:, :128]
            u = st[:, 128:]
            first = info_ref[0] == 0
            pay_ref[h] = jnp.where(first, u, jnp.concatenate([t[:64], u[:64]], axis=0))
            keep_ref[h] = jnp.concatenate([t[64:], u[64:]], axis=0)
        return c

    lax.fori_loop(0, 8 // HEADS_PER_STEP, solve, 0)


HEADS_PER_STEP = 4


def vm():
    return pl.BlockSpec(memory_space=pltpu.VMEM)


def sm():
    return pl.BlockSpec(memory_space=pltpu.SMEM)


def maps(info, k, v, g, b):
    big = lambda *s: pltpu.VMEM(s, F32)
    return pl.pallas_call(
        maps_kernel,
        out_shape=[
            jax.ShapeDtypeStruct((8, 128, 128), F32),
            jax.ShapeDtypeStruct((8, 128, 128), F32),
            jax.ShapeDtypeStruct((8, 256, 256), F32),
        ],
        in_specs=[sm(), vm(), vm(), vm(), vm()],
        out_specs=[vm(), vm(), vm()],
        scratch_shapes=[
            big(1024, 128), big(2048, 128),
            big(8, 256, 128), big(8, 256, 128), big(8, 256, 128), big(8, 256, 128),
            big(8, 8, 256), big(8, 8, 128),
            big(8, 128, 128), big(8, 128, 128), big(8, 128, 128),
            big(2, 256, 128), big(2, 256, 128),
        ],
        compiler_params=pltpu.CompilerParams(vmem_limit_bytes=48 * 2**20),
        name="maps",
    )(info, k, v, g, b)


def final_kernel(info_ref, pay_ref, keep_ref, got_ref, out_ref):
    def work(a_ref, m_ref):
        for h in range(8):
            out_ref[pl.ds(h * 64, 64), :] = mm_small(a_ref[h, :64], m_ref[h]) + a_ref[h, 64:]

    @pl.when(info_ref[0] == 0)
    def _():
        work(got_ref, pay_ref)

    @pl.when(info_ref[0] != 0)
    def _():
        work(keep_ref, got_ref)


def final(info, pay, keep, got):
    return pl.pallas_call(
        final_kernel,
        out_shape=jax.ShapeDtypeStruct((512, 128), F32),
        in_specs=[sm(), vm(), vm(), vm()],
        out_specs=vm(),
        compiler_params=pltpu.CompilerParams(vmem_limit_bytes=32 * 2**20),
        name="final",
    )(info, pay, keep, got)


def reads_kernel(info_ref, q_ref, k_ref, g_ref, y_ref, m_ref, o_ref, qf, kf, pcol, ecol, brow, of):
    qf[...] = q_ref[...].astype(F32)
    kf[...] = k_ref[...].astype(F32)
    G = decay_rows(g_ref[...], live_lanes(info_ref))
    cols = to_columns(G)
    lane = lax.broadcasted_iota(jnp.int32, (256, 128), 1)
    norms = jnp.zeros((256, 128), F32)
    for kh in range(4):
        norms = jnp.where(lane == kh, log_norm(kf[pl.ds(kh, 256, stride=4), :]), norms)
        norms = jnp.where(lane == 4 + kh, log_norm(qf[pl.ds(kh, 256, stride=4), :]), norms)
    norm_rows = norms.T
    for h in range(8):
        kh = h // 2
        p = cols[:, h : h + 1] + norms[:, 4 + kh : 5 + kh]
        pcol[h] = jnp.broadcast_to(p, (256, 128))
        ecol[h] = jnp.broadcast_to(jnp.exp(p), (256, 128))
        brow[h] = jnp.broadcast_to(G[h : h + 1, :] - norm_rows[kh : kh + 1, :], (8, 256))

    row = lax.broadcasted_iota(jnp.int32, (128, 128), 0)
    col = lax.broadcasted_iota(jnp.int32, (128, 128), 1)
    lower = row >= col
    has = (info_ref[0] != 0).astype(F32)
    live1 = info_ref[1] * 128 > info_ref[0] * 256
    live2 = info_ref[1] * 128 > info_ref[0] * 256 + 128

    def one(kh, c):
        k = kf[pl.ds(kh, 256, stride=4), :].astype(BF16)
        q = qf[pl.ds(kh, 256, stride=4), :].astype(BF16)
        qk1 = mm_nt(q[:128], k[:128])
        qk2 = mm_nt(q[128:], k)
        for s in range(2):
            h = 2 * kh + s
            m = m_ref[h] * has
            mh, ml = split(m)
            mrow = jnp.concatenate([mh, ml], axis=1)
            mpack = jnp.concatenate([mrow, mrow], axis=0)
            w = y_ref[h, :, :128]
            u = y_ref[h, :, 128:]
            d = u - fold(mm(pack_left(w), mpack))
            qm = fold(mm(q, mrow)) * ecol[h]
            p1, p2 = pcol[h, :128], pcol[h, 128:]
            b1, b2 = brow[h, 0:1, :128], brow[h, 0:1, 128:]
            p11 = jnp.where(lower, jnp.exp(p1 - b1) * qk1, 0.0)
            p21 = jnp.exp(p2 - b1) * qk2[:, :128]
            p22 = jnp.where(lower, jnp.exp(p2 - b2) * qk2[:, 128:], 0.0)
            o1 = qm[:128] + mm_small(p11, d[:128])
            ph, pl_ = split(jnp.concatenate([p21, p22], axis=1))
            dh, dl = split(d)
            o2 = qm[128:] + fold(mm(ph, jnp.concatenate([dh, dl], axis=1))) + mm(pl_, dh)
            o1 = jnp.where(live1, o1, 0.0)
            o2 = jnp.where(live2, o2, 0.0)
            of[pl.ds(h, 256, stride=8), :] = jnp.concatenate([o1, o2], axis=0)
        return c

    lax.fori_loop(0, 4, one, 0)
    o_ref[...] = of[...].astype(BF16)


def reads(info, q, k, g, y, m):
    big = lambda *s: pltpu.VMEM(s, F32)
    return pl.pallas_call(
        reads_kernel,
        out_shape=jax.ShapeDtypeStruct((2048, 128), BF16),
        in_specs=[sm(), vm(), vm(), vm(), vm(), vm()],
        out_specs=vm(),
        scratch_shapes=[
            big(1024, 128), big(1024, 128), big(8, 256, 128), big(8, 256, 128),
            big(8, 8, 256), big(2048, 128),
        ],
        compiler_params=pltpu.CompilerParams(vmem_limit_bytes=48 * 2**20),
        cost_estimate=pl.CostEstimate(flops=8 * 4 * 2 * 256**3, bytes_accessed=4 * 2**20, transcendentals=0),
        name="reads",
    )(info, q, k, g, y, m)


def reorder_kernel(slot_ref, in_ref, out_ref):
    for s in range(32):
        out_ref[slot_ref[s]] = in_ref[s]


def reorder(slot_map, x):
    return pl.pallas_call(
        reorder_kernel,
        out_shape=jax.ShapeDtypeStruct(x.shape, x.dtype),
        in_specs=[sm(), vm()],
        out_specs=vm(),
        name="reorder",
    )(slot_map, x)


def local(queries, keys, values, gate_logit, beta_logit, token_blocks, slot_map):
    q = queries.reshape(1024, 128)
    k = keys.reshape(1024, 128)
    v = values.reshape(2048, 128)
    g = gate_logit.reshape(8, 256)
    b = beta_logit.reshape(8, 256)
    ctx = lax.axis_index("ctx").astype(jnp.int32)
    info = jnp.stack([ctx, token_blocks[0]])
    pay, keep, y = maps(info, k, v, g, b)
    got = lax.ppermute(pay, "ctx", [(0, 1), (1, 0)])
    rows = final(info, pay, keep, got)
    spread = lax.all_to_all(rows.reshape(32, 16, 128), "sess", 0, 0, tiled=True)
    out = reads(info, q, k, g, y, got)
    back = lax.all_to_all(reorder(slot_map, spread), "sess", 0, 0, tiled=True)
    return out.reshape(1, 256, 8, 128), back.reshape(1, 8, 64, 128)


def solution(mesh):
    from jax.sharding import PartitionSpec as P
    placed = (
        P("sess", "ctx", "head", None), P("sess", "ctx", "head", None), P("sess", "ctx", "head", None),
        P("sess", "head", "ctx"), P("sess", "head", "ctx"), P("sess"), P(),
    )
    return jax.shard_map(
        local, mesh=mesh, in_specs=placed,
        out_specs=(P("sess", "ctx", "head", None), P("sess", "head", "ctx", None)),
        check_vma=False,
    )
```

time: 398 us -> 69.6 us (0.17)
  other arithmetic: 167 us -> 0.08 us
  waiting for transfers between devices: 161 us -> 8.59 us
  matrix products: 46.5 us -> 0 us
  Pallas kernels: 0 us -> 26.5 us
  blocking collectives: 0 us -> 24.6 us
  between operations: 14.7 us -> 1.34 us
    another operation x5 -> x1, other arithmetic: 159 us -> 0.08 us  [local(): info = jnp.stack([ctx, token_blocks[0]])]
    all_gather x3 -> x0, waiting for transfers between devices: 127 us -> none  [the longest x1 99 us: local(): collected = lax.all_gather(final_rows, 'sess', axis=0, tiled=True)]
    dot_general x21 -> x0, matrix products: 44.7 us -> none  [the longest x1 11.1 us: local(): jnp.einsum('ln,nhrd->lhrd', pick, collected, precision=HIGH_PRECISION)]
    psum x1 -> x0, waiting for transfers between devices: 32.6 us -> none  [spread_2(): return lax.psum(jnp.where(mine, x, jnp.zeros_like(x)), axis)]
    pallas_call x0 -> x4, Pallas kernels: none -> 26.5 us  [the longest x1 18.4 us: maps(): pl.pallas_call(maps_kernel, out_shape=[jax.ShapeDtypeStruct((8, 128, 128)...]
    all_to_all x0 -> x1, blocking collectives: none -> 24.6 us  [local(): spread = lax.all_to_all(rows.reshape(32, 16, 128), 'sess', 0, 0, tiled=True)]
    all_to_all x0 -> x1, waiting for transfers between devices: none -> 6.69 us  [local(): back = lax.all_to_all(reorder(slot_map, spread), 'sess', 0, 0, tiled=True)]
  transfers between devices with their start and end apart: 4 -> 2, of which waited for: 4 -> 2; matrix products, arithmetic and copies ran while one was open for 2% -> 0% of each run, Pallas kernels for 0% -> 8%
where the time goes in v1:
time: 69.6 us; the launch traced here: 69.2 us
  Pallas kernels  26.5 us (38%)
  blocking collectives  24.6 us (35%)
  waiting for transfers between devices  8.59 us (12%)
  local copies, waits for them, and re-layouts  4.1 us (6%)
  starting transfers between devices  3.96 us (6%)
  between operations  1.34 us (2%)
    all_to_all x1, blocking collectives, local(): spread = lax.all_to_all(rows.reshape(32, 16, 128), 'sess', 0, 0, tiled=True)  24.6 us
    pallas_call x1, Pallas kernels, maps(): pl.pallas_call(maps_kernel, out_shape=[jax.ShapeDtypeStruct((8, 128, 128)...  18.4 us
    all_to_all x1, waiting for transfers between devices, local(): back = lax.all_to_all(reorder(slot_map, spread), 'sess', 0, 0, tiled=True)  6.69 us
    pallas_call x1, Pallas kernels, reads(): pl.pallas_call(reads_kernel, out_shape=jax.ShapeDtypeStruct((2048, 128),...  5.59 us
    unnamed x15, local copies, waits for them, and re-layouts  4.1 us
    all_to_all x1, starting transfers between devices, local(): back = lax.all_to_all(reorder(slot_map, spread), 'sess', 0, 0, tiled=True)  3.87 us
    ppermute x1, waiting for transfers between devices, local(): got = lax.ppermute(pay, 'ctx', [(0, 1), (1, 0)])  1.9 us
    pallas_call x1, Pallas kernels, reorder(): pl.pallas_call(reorder_kernel, out_shape=jax.ShapeDtypeStruct(x.shape, x....  1.69 us
  transfers between devices with their start and end apart: 2, of which 2 were waited for; matrix products, arithmetic and copies ran while one was open for 0% of the time, Pallas kernels for 8%

profile of v1, /device:TPU:6, one launch (start us, length us, event | category | flops | bytes accessed | tf_op | source)
XLA Modules:
  0.0 69.2 jit_solution(4472803197869219382)
XLA Ops:
  1.3 0.1 pad_add_fusion.info_ref
  1.4 0.0 copy-start
  1.4 1.0 %copy-done = bf16[1,256,8,128]{3,2,1,0:T(8,128)(2,1)S(1)} copy-done((bf16[1,256,8,128]{3,2,1,0:T(8,128)(2,1)S(1)}, bf16[1,256,8,128]{3,2,1,0:T(8,128)(2,1)}, u32[]{:S(2)}) %copy-start) | copy-done | bytes 524312
  2.4 0.0 copy-start.1
  2.4 0.9 %copy-done.1 = bf16[1,256,4,128]{3,2,1,0:T(4,128)(2,1)S(1)} copy-done((bf16[1,256,4,128]{3,2,1,0:T(4,128)(2,1)S(1)}, bf16[1,256,4,128]{3,2,1,0:T(4,128)(2,1)}, u32[]{:S(2)}) %copy-start.1) | copy-done | bytes 262168
  3.3 0.0 copy-start.3
  3.3 0.7 %copy-done.3 = f32[1,8,256]{2,1,0:T(8,128)S(1)} copy-done((f32[1,8,256]{2,1,0:T(8,128)S(1)}, f32[1,8,256]{2,1,0:T(8,128)}, u32[]{:S(2)}) %copy-start.3) | copy-done | bytes 8216
  4.0 0.0 copy-start.4
  4.0 0.7 %copy-done.4 = f32[1,8,256]{2,1,0:T(8,128)S(1)} copy-done((f32[1,8,256]{2,1,0:T(8,128)S(1)}, f32[1,8,256]{2,1,0:T(8,128)}, u32[]{:S(2)}) %copy-start.4) | copy-done | bytes 8216
  4.7 0.0 copy-start.2
  4.7 0.0 copy-start.5
  4.7 0.0 copy-start.6
  4.7 18.4 %maps.1 = (f32[8,128,128]{2,1,0:T(8,128)S(1)}, f32[8,128,128]{2,1,0:T(8,128)S(1)}, f32[8,256,256]{2,1,0:T(8,128)S(1)}) custom-call(s32[2]{0:T(128)S(1)} %pad_add_fusion.info_ref, bf16[1024,128]{1,0:T(8,128)(2,1)S(1)} %bitcast.11, bf16[2048,128]{1,0:T(8,128)(2,1)S(1)} %bitcast.10, f32[8,256]{1,0:T(8,128)S(1)} %bitcast.14, f32[8,256]{1,0:T(8,128)S(1)} %bitcast.13), custom_call_target="tpu_custom_call" | custom-call | tf_op jit(solution)/shard_map/maps/pallas_call | solution.py:209
  23.1 0.1 collective-permute-start
  23.2 1.9 %collective-permute-done.m_ref.got_ref = f32[8,128,128]{2,1,0:T(8,128)S(1)} collective-permute-done((f32[8,128,128]{2,1,0:T(8,128)S(1)}, f32[8,128,128]{2,1,0:T(8,128)S(1)}, u32[]{:S(2)}, u32[]{:S(2)}) %collective-permute-start) | collective-permute-done | bytes 524320 | tf_op jit(solution)/shard_map/ppermute | solution.py:354
  25.1 0.9 %final.1 = f32[512,128]{1,0:T(8,128)S(1)} custom-call(s32[2]{0:T(128)S(1)} %pad_add_fusion.info_ref, f32[8,128,128]{2,1,0:T(8,128)S(1)} %get-tuple-element.6.pay_ref, f32[8,128,128]{2,1,0:T(8,128)S(1)} %get-tuple-element.7.keep_ref, f32[8,128,128]{2,1,0:T(8,128)S(1)} %collective-permute-done.m_ref.got_ref), custom_call_target="tpu_custom_call" | custom-call | tf_op jit(solution)/shard_map/final/pallas_call | solution.py:245
  26.0 24.6 %all_to_all.10.in_ref = f32[32,16,128]{2,1,0:T(8,128)} all-to-all(f32[32,16,128]{2,1,0:T(8,128)S(1)} %bitcast.9), channel_id=1, replica_groups=mesh['ctx'=2,'head'=4,'sess'=32] {'sess'}, dimensions={0} | all-to-all | bytes 524288 | tf_op jit(solution)/shard_map/all_to_all | solution.py:356
  50.6 1.7 %reorder.1 = f32[32,16,128]{2,1,0:T(8,128)} custom-call(s32[32]{0:T(128)} %slot_ref.1, f32[32,16,128]{2,1,0:T(8,128)} %all_to_all.10.in_ref), custom_call_target="tpu_custom_call" | custom-call | tf_op jit(solution)/shard_map/reorder/pallas_call | solution.py:336
  52.3 3.9 %all-to-all-start.1 = ((f32[32,16,128]{2,1,0:T(8,128)}), f32[32,16,128]{2,1,0:T(8,128)S(1)}, u32[]{:S(2)}, u32[]{:S(2)}) async-start(f32[32,16,128]{2,1,0:T(8,128)} %reorder.1), calls=%async_computation.1 | async-start | bytes 524288 | tf_op jit(solution)/shard_map/all_to_all | solution.py:358
  56.2 0.0 copy-done.2
  56.2 0.0 copy-done.5
  56.2 0.0 copy-done.6
  56.2 5.6 %reads.1 = bf16[2048,128]{1,0:T(8,128)(2,1)} custom-call(s32[2]{0:T(128)S(1)} %pad_add_fusion.info_ref, bf16[1024,128]{1,0:T(8,128)(2,1)S(1)} %bitcast.16, bf16[1024,128]{1,0:T(8,128)(2,1)S(1)} %bitcast.12, f32[8,256]{1,0:T(8,128)S(1)} %bitcast.15, f32[8,256,256]{2,1,0:T(8,128)S(1)} %get-tuple-element.5.y_ref, ...), custom_call_target="tpu_custom_call" | custom-call | flops 1073741824 | bytes 4194304 | tf_op jit(solution)/shard_map/reads/pallas_call | solution.py:315
  61.8 6.7 %all-to-all-done.1 = f32[32,16,128]{2,1,0:T(8,128)S(1)} async-done(((f32[32,16,128]{2,1,0:T(8,128)}), f32[32,16,128]{2,1,0:T(8,128)S(1)}, u32[]{:S(2)}, u32[]{:S(2)}) %all-to-all-start.1) | async-done | bytes 262176 | tf_op jit(solution)/shard_map/all_to_all | solution.py:358
  68.5 0.7 %copy.11 = f32[1,8,64,128]{3,2,1,0:T(8,128)} copy(f32[1,8,64,128]{3,2,1,0:T(8,128)S(1)} %bitcast.17) | data formatting | bytes 524288
Async XLA Ops:
  1.4 1.0 %copy-start = (bf16[1,256,8,128]{3,2,1,0:T(8,128)(2,1)S(1)}, bf16[1,256,8,128]{3,2,1,0:T(8,128)(2,1)}, u32[]{:S(2)}) copy-start(bf16[1,256,8,128]{3,2,1,0:T(8,128)(2,1)} %param.9) | copy-start | bytes 1572868
  2.4 0.9 %copy-start.1 = (bf16[1,256,4,128]{3,2,1,0:T(4,128)(2,1)S(1)}, bf16[1,256,4,128]{3,2,1,0:T(4,128)(2,1)}, u32[]{:S(2)}) copy-start(bf16[1,256,4,128]{3,2,1,0:T(4,128)(2,1)} %param.8) | copy-start | bytes 786436
  3.3 0.7 %copy-start.3 = (f32[1,8,256]{2,1,0:T(8,128)S(1)}, f32[1,8,256]{2,1,0:T(8,128)}, u32[]{:S(2)}) copy-start(f32[1,8,256]{2,1,0:T(8,128)} %param.11) | copy-start | bytes 24580
  4.0 0.7 %copy-start.4 = (f32[1,8,256]{2,1,0:T(8,128)S(1)}, f32[1,8,256]{2,1,0:T(8,128)}, u32[]{:S(2)}) copy-start(f32[1,8,256]{2,1,0:T(8,128)} %param.10) | copy-start | bytes 24580
  4.7 51.4 %copy-start.2 = (bf16[1,256,4,128]{3,2,1,0:T(4,128)(2,1)S(1)}, bf16[1,256,4,128]{3,2,1,0:T(4,128)(2,1)}, u32[]{:S(2)}) copy-start(bf16[1,256,4,128]{3,2,1,0:T(4,128)(2,1)} %param.8) | copy-start | bytes 786436
  4.7 51.4 %copy-start.5 = (f32[1,8,256]{2,1,0:T(8,128)S(1)}, f32[1,8,256]{2,1,0:T(8,128)}, u32[]{:S(2)}) copy-start(f32[1,8,256]{2,1,0:T(8,128)} %param.10) | copy-start | bytes 24580
  4.7 51.4 %copy-start.6 = (bf16[1,256,4,128]{3,2,1,0:T(4,128)(2,1)S(1)}, bf16[1,256,4,128]{3,2,1,0:T(4,128)(2,1)}, u32[]{:S(2)}) copy-start(bf16[1,256,4,128]{3,2,1,0:T(4,128)(2,1)} %param.7) | copy-start | bytes 786436
  23.1 2.0 %collective-permute-start = (f32[8,128,128]{2,1,0:T(8,128)S(1)}, f32[8,128,128]{2,1,0:T(8,128)S(1)}, u32[]{:S(2)}, u32[]{:S(2)}) collective-permute-start(f32[8,128,128]{2,1,0:T(8,128)S(1)} %get-tuple-element.6.pay_ref), channel_id=1, source_target_pairs={{0,128},{128,0},{1,129},{129,1},{2,130},{130,2},{3,131},{131,3},{4... | collective-permute-start | bytes 1572872 | tf_op jit(solution)/shard_map/ppermute | solution.py:354
  52.3 16.2 %all-to-all-start.1 = ((f32[32,16,128]{2,1,0:T(8,128)}), f32[32,16,128]{2,1,0:T(8,128)S(1)}, u32[]{:S(2)}, u32[]{:S(2)}) async-start(f32[32,16,128]{2,1,0:T(8,128)} %reorder.1), calls=%async_computation.1 | async-start | bytes 524288 | tf_op jit(solution)/shard_map/all_to_all | solution.py:358

commit v2 on v1

v2 whole, which is shorter than its diff:
```python
import functools
import jax
import jax.numpy as jnp
from jax import lax
from jax.experimental import pallas as pl
from jax.experimental.pallas import tpu as pltpu

F32 = jnp.float32
BF16 = jnp.bfloat16


def split(x):
    hi = x.astype(BF16)
    return hi, (x - hi.astype(F32)).astype(BF16)


def mm(a, b):
    return jnp.dot(a, b, preferred_element_type=F32)


def mm_nt(a, b):
    return lax.dot_general(a, b, (((1,), (1,)), ((), ())), preferred_element_type=F32)


def pack_left(a):
    hi, lo = split(a)
    return jnp.concatenate([hi, lo], axis=1)


def pack_right(b):
    hi, lo = split(b)
    row = jnp.concatenate([hi, lo], axis=1)
    return jnp.concatenate([row, row], axis=0)


def fold(r):
    return r[:, :128] + r[:, 128:]


def mm_small(a, b):
    return fold(mm(pack_left(a), pack_right(b)))


def mm_wide(a, b):
    ah, al = split(a)
    bh, bl = split(b)
    return mm(jnp.concatenate([ah, al], axis=1), jnp.concatenate([bh, bh], axis=0)) + mm(ah, bl)


def decay_rows(gate, live):
    x = jnp.where(live, -(jnp.maximum(gate, 0.0) + jnp.log1p(jnp.exp(-jnp.abs(gate)))), 0.0)
    lane = lax.broadcasted_iota(jnp.int32, x.shape, 1)
    step = 1
    while step < 256:
        x = x + jnp.where(lane >= step, pltpu.roll(x, step, 1), 0.0)
        step *= 2
    return x


def to_columns(rows):
    pad = jnp.zeros((128 - rows.shape[0], 256), F32)
    return jnp.concatenate([rows, pad], axis=0).T


def live_lanes(info_ref):
    edge = info_ref[1] * 128 - info_ref[0] * 256
    return lax.broadcasted_iota(jnp.int32, (8, 256), 1) < edge


def log_norm(x):
    return -0.5 * jnp.log(jnp.sum(x * x, axis=1, keepdims=True) + 1e-06)


def split3(x):
    hi = x.astype(BF16)
    r = x - hi.astype(F32)
    mid = r.astype(BF16)
    lo = (r - mid.astype(F32)).astype(BF16)
    return hi, mid, lo


def mm_tn(a, b):
    return lax.dot_general(a, b, (((0,), (0,)), ((), ())), preferred_element_type=F32)


def twice(pair):
    row = jnp.concatenate(pair, axis=1)
    return jnp.concatenate([row, row], axis=0)


def picked(x, b, odd):
    return jnp.concatenate([x[i : i + b] for i in range(odd * b, 128, 2 * b)], axis=0)


def woven(even, odd, b):
    parts = []
    for i in range(0, 64, b):
        parts += [even[i : i + b], odd[i : i + b]]
    return jnp.concatenate(parts, axis=0)


def log_beta(x):
    return -(jnp.maximum(-x, 0.0) + jnp.log1p(jnp.exp(-jnp.abs(x))))


def spans(left, right):
    ones = jnp.ones((24, 256), F32)
    lhs = jnp.concatenate([p.astype(F32) for p in split3(left)] + [ones, jnp.zeros((80, 256), F32)], axis=0)
    cols = lhs.T.astype(BF16)
    rhs = jnp.concatenate([ones.astype(F32)] + [p.astype(F32) for p in split3(-right)] + [jnp.zeros((80, 256), F32)], axis=0)
    at = lax.broadcasted_iota(jnp.int32, (128, 256), 0) % 8
    return cols, lambda h: jnp.where(at == h, rhs, 0.0).astype(BF16)


def maps_kernel(
    tb_hbm, k_hbm, v_hbm, g_hbm, b_hbm, pay_ref, keep_ref, x_ref, l21,
    tb, kr, vr, gr, br, kf, vf, kks, kt, rows, l11, l22, cmp_ref, xc, sems,
):
    copies = [
        pltpu.make_async_copy(src, dst, sems.at[i])
        for i, (src, dst) in enumerate(
            [(tb_hbm, tb), (k_hbm, kr), (g_hbm, gr), (b_hbm, br), (v_hbm, vr)]
        )
    ]
    for c in copies:
        c.start()
    ctx = lax.axis_index("ctx")
    row = lax.broadcasted_iota(jnp.int32, (128, 128), 0)
    col = lax.broadcasted_iota(jnp.int32, (128, 128), 1)
    lower = row > col
    eye = row == col
    copies[1].wait()
    kf[...] = kr[...].astype(F32)
    norms = []
    for kh in range(4):
        kx = kf[pl.ds(kh, 256, stride=4), :]
        k = kx.astype(BF16)
        kt[kh] = kx.T
        kk1 = mm_nt(k[:128], k[:128])
        kk2 = mm_nt(k[128:], k)
        kks[kh, :128, :128] = kk1
        kks[kh, 128:] = kk2
        s1 = jnp.sum(jnp.where(eye, kk1, 0.0), axis=0, keepdims=True)
        s2 = jnp.sum(jnp.where(eye, kk2[:, 128:], 0.0), axis=0, keepdims=True)
        norms.append(jnp.concatenate([s1, s2], axis=1))
    ln = -0.5 * jnp.log(jnp.concatenate([norms[h // 2] for h in range(8)], axis=0) + 1e-06)
    copies[0].wait()
    copies[2].wait()
    copies[3].wait()
    edge = tb[0] * 128 - ctx * 256
    live = lax.broadcasted_iota(jnp.int32, (8, 256), 1) < edge
    G = decay_rows(gr[...], live)
    a = G + ln + jnp.where(live, log_beta(br[...]), -1e4)
    last = G[:, 255:256]
    rows[0] = jnp.exp(a)
    rows[1] = jnp.where(live, jnp.exp(log_beta(br[...])), 0.0)
    rows[2] = jnp.exp(last - G + ln)
    rows[3] = jnp.broadcast_to(jnp.exp(last), (8, 256))
    cols, right = spans(a, G - ln)
    for h in range(8):
        kh = h // 2
        r = right(h)
        d1 = mm(cols[:128], r[:, :128])
        d2 = mm(cols[128:], r)
        l11[h] = jnp.where(lower, jnp.exp(d1) * kks[kh, :128, :128], 0.0)
        l21[h] = jnp.exp(d2[:, :128]) * kks[kh, 128:, :128]
        l22[h] = jnp.where(lower, jnp.exp(d2[:, 128:]) * kks[kh, 128:, 128:], 0.0)

    group = lax.broadcasted_iota(jnp.int32, (16, 128), 1) // 16
    for kb in range(16):
        src = l11 if kb < 8 else l22
        r0 = (kb % 8) * 16
        acc = jnp.zeros((16, 128), F32)
        for q in range(8):
            t = src[q, r0 : r0 + 16, :]
            shift = (q * 16 - r0) % 128
            if shift:
                t = pltpu.roll(t, shift, 1)
            acc = jnp.where(group == q, t, acc)
        cmp_ref[kb * 16 : kb * 16 + 16, :] = acc

    lane = lax.broadcasted_iota(jnp.int32, (16, 128), 1)
    base = (lane // 16) * 16
    xs = [jnp.where(lane % 16 == i, 1.0, 0.0).astype(F32) for i in range(16)]
    ls = [cmp_ref[pl.ds(i, 16, stride=16), :] for i in range(16)]
    for j in range(16):
        xc[pl.ds(j, 16, stride=16), :] = xs[j]
        for i in range(j + 1, 16):
            coef = jnp.take_along_axis(ls[i], base + j, axis=1, mode="promise_in_bounds")
            xs[i] = xs[i] - coef * xs[j]

    block = row // 16 == col // 16
    for h in range(8):
        for part, src in ((0, l11), (1, l22)):
            x = xc[part * 128 : part * 128 + 128, :]
            x = jnp.take_along_axis(x, h * 16 + col % 16, axis=1, mode="promise_in_bounds")
            x_ref[h, part] = jnp.where(block, x, 0.0)
    halfrow = lax.broadcasted_iota(jnp.int32, (64, 128), 0)
    halfcol = lax.broadcasted_iota(jnp.int32, (64, 128), 1)
    for b in (16, 32, 64):
        under = halfcol // b == (halfrow // b) * 2
        for h in range(8):
            for part, src in ((0, l11), (1, l22)):
                x = x_ref[h, part]
                l = jnp.where(under, picked(src[h], b, 1), 0.0)
                m = fold(mm(pack_left(l), pack_right(x)))
                zero = jnp.zeros((64, 128), BF16)
                mh, ml = split(m)
                odd = picked(x, b, 1)
                right_m = twice([woven(zero, mh, b), woven(zero, ml, b)])
                odd = odd - fold(mm(pack_left(odd), right_m))
                x_ref[h, part] = woven(picked(x, b, 0), odd, b)

    copies[4].wait()
    vf[...] = vr[...].astype(F32)
    for h in range(8):
        kh = h // 2
        k = kf[pl.ds(kh, 256, stride=4), :].astype(BF16)
        v = vf[pl.ds(h, 256, stride=8), :].astype(BF16)
        ktz = kt[kh] * rows[2, h : h + 1, :]
        b2 = mm_small(ktz[:, 128:], x_ref[h, 1])
        b1 = mm_small(ktz[:, :128] - mm_small(b2, l21[h]), x_ref[h, 0])
        bb = jnp.concatenate([b1, b2], axis=1)
        t = mm(jnp.concatenate(split(bb * rows[0, h : h + 1, :]), axis=0), k)
        u = mm(jnp.concatenate(split(bb * rows[1, h : h + 1, :]), axis=0), v)
        t = jnp.where(eye, rows[3, h : h + 1, :128], 0.0) - (t[:128] + t[128:])
        u = u[:128] + u[128:]
        pay_ref[h] = jnp.where(ctx == 0, u, jnp.concatenate([t[:64], u[:64]], axis=0))
        keep_ref[h] = jnp.concatenate([t[64:], u[64:]], axis=0)


HEADS_PER_STEP = 4


def vm():
    return pl.BlockSpec(memory_space=pltpu.VMEM)


def sm():
    return pl.BlockSpec(memory_space=pltpu.SMEM)


def hbm():
    return pl.BlockSpec(memory_space=pltpu.HBM)


VL = 60


def maps(tb, k, v, g, b):
    big = lambda *s: pltpu.VMEM(s, F32)
    return pl.pallas_call(
        maps_kernel,
        out_shape=[
            jax.ShapeDtypeStruct((8, 128, 128), F32),
            jax.ShapeDtypeStruct((8, 128, 128), F32),
            jax.ShapeDtypeStruct((8, 2, 128, 128), F32),
            jax.ShapeDtypeStruct((8, 128, 128), F32),
        ],
        in_specs=[hbm()] * 5,
        out_specs=[vm()] * 4,
        scratch_shapes=[
            pltpu.SMEM((1,), jnp.int32),
            pltpu.VMEM((1024, 128), BF16), pltpu.VMEM((2048, 128), BF16), big(8, 256), big(8, 256),
            big(1024, 128), big(2048, 128), big(4, 256, 256), big(4, 128, 256), big(4, 8, 256),
            big(8, 128, 128), big(8, 128, 128),
            big(256, 128), big(256, 128),
            pltpu.SemaphoreType.DMA((5,)),
        ],
        compiler_params=pltpu.CompilerParams(vmem_limit_bytes=VL * 2**20),
        name="maps",
    )(tb, k, v, g, b)


def final_kernel(pay_ref, keep_ref, got_ref, out_ref):
    def work(a_ref, m_ref):
        for h in range(8):
            out_ref[pl.ds(h * 64, 64), :] = mm_small(a_ref[h, :64], m_ref[h]) + a_ref[h, 64:]

    first = lax.axis_index("ctx") == 0

    @pl.when(first)
    def _():
        work(got_ref, pay_ref)

    @pl.when(jnp.logical_not(first))
    def _():
        work(keep_ref, got_ref)


def final(pay, keep, got):
    return pl.pallas_call(
        final_kernel,
        out_shape=jax.ShapeDtypeStruct((512, 128), F32),
        in_specs=[vm(), vm(), vm()],
        out_specs=vm(),
        compiler_params=pltpu.CompilerParams(vmem_limit_bytes=32 * 2**20),
        name="final",
    )(pay, keep, got)


def reads_kernel(tb, q_ref, k_ref, v_ref, g_ref, b_ref, x_ref, l_ref, m_ref, o_ref, qf, kf, vf, rcol, bcol, ecol, of):
    qf[...] = q_ref[...].astype(F32)
    kf[...] = k_ref[...].astype(F32)
    vf[...] = v_ref[...].astype(F32)
    ctx = lax.axis_index("ctx")
    edge = tb[0] * 128 - ctx * 256
    live = lax.broadcasted_iota(jnp.int32, (8, 256), 1) < edge
    G = decay_rows(g_ref[...], live)
    lb = log_beta(b_ref[...])
    lane = lax.broadcasted_iota(jnp.int32, (256, 128), 1)
    norms = jnp.zeros((256, 128), F32)
    for kh in range(4):
        nk = log_norm(kf[pl.ds(kh, 256, stride=4), :])
        nq = log_norm(qf[pl.ds(kh, 256, stride=4), :])
        for h in (2 * kh, 2 * kh + 1):
            norms = jnp.where(lane == h, nk, norms)
            norms = jnp.where(lane == 8 + h, nq, norms)
    norm_rows = norms.T
    nk, nq = norm_rows[:8], norm_rows[8:16]
    p = G + nq
    a = G + nk + jnp.where(live, lb, -1e4)
    scale = to_columns(jnp.concatenate([jnp.exp(a), jnp.where(live, jnp.exp(lb), 0.0), jnp.exp(p)], axis=0))
    for h in range(8):
        rcol[h] = jnp.broadcast_to(scale[:, h : h + 1], (256, 128))
        bcol[h] = jnp.broadcast_to(scale[:, 8 + h : 9 + h], (256, 128))
        ecol[h] = jnp.broadcast_to(scale[:, 16 + h : 17 + h], (256, 128))
    cols, right = spans(p, G - nk)
    row = lax.broadcasted_iota(jnp.int32, (128, 128), 0)
    col = lax.broadcasted_iota(jnp.int32, (128, 128), 1)
    lower = row >= col
    has = (ctx != 0).astype(F32)
    live1, live2 = edge > 0, edge > 128
    for kh in range(4):
        k = kf[pl.ds(kh, 256, stride=4), :].astype(BF16)
        q = qf[pl.ds(kh, 256, stride=4), :].astype(BF16)
        qk1 = mm_nt(q[:128], k[:128])
        qk2 = mm_nt(q[128:], k)
        kq = jnp.concatenate([k, q], axis=0)
        for h in (2 * kh, 2 * kh + 1):
            mrow = jnp.concatenate(split(m_ref[h] * has), axis=1)
            km = fold(mm(kq, mrow))
            d = bcol[h] * vf[pl.ds(h, 256, stride=8), :] - rcol[h] * km[:256]
            d1 = mm_small(x_ref[h, 0], d[:128])
            d2 = mm_small(x_ref[h, 1], d[128:] - mm_small(l_ref[h], d1))
            qm = km[256:] * ecol[h]
            r = right(h)
            e1 = mm(cols[:128], r[:, :128])
            e2 = mm(cols[128:], r)
            p11 = jnp.where(lower, jnp.exp(e1) * qk1, 0.0)
            p21 = jnp.exp(e2[:, :128]) * qk2[:, :128]
            p22 = jnp.where(lower, jnp.exp(e2[:, 128:]) * qk2[:, 128:], 0.0)
            o1 = qm[:128] + mm_small(p11, d1)
            ph, pl_ = split(jnp.concatenate([p21, p22], axis=1))
            dh, dl = split(jnp.concatenate([d1, d2], axis=0))
            o2 = qm[128:] + fold(mm(ph, jnp.concatenate([dh, dl], axis=1))) + mm(pl_, dh)
            o1 = jnp.where(live1, o1, 0.0)
            o2 = jnp.where(live2, o2, 0.0)
            of[pl.ds(h, 256, stride=8), :] = jnp.concatenate([o1, o2], axis=0)
    o_ref[...] = of[...].astype(BF16)


def reads(tb, q, k, v, g, b, x, l, m):
    big = lambda *s: pltpu.VMEM(s, F32)
    return pl.pallas_call(
        reads_kernel,
        out_shape=jax.ShapeDtypeStruct((2048, 128), BF16),
        in_specs=[sm()] + [vm()] * 8,
        out_specs=vm(),
        scratch_shapes=[
            big(1024, 128), big(1024, 128), big(2048, 128),
            big(8, 256, 128), big(8, 256, 128), big(8, 256, 128), big(2048, 128),
        ],
        compiler_params=pltpu.CompilerParams(vmem_limit_bytes=40 * 2**20),
        cost_estimate=pl.CostEstimate(flops=8 * 4 * 2 * 256**3, bytes_accessed=4 * 2**20, transcendentals=0),
        name="reads",
    )(tb, q, k, v, g, b, x, l, m)


def local(queries, keys, values, gate_logit, beta_logit, token_blocks, slot_map):
    q = queries.reshape(1024, 128)
    k = keys.reshape(1024, 128)
    v = values.reshape(2048, 128)
    g = gate_logit.reshape(8, 256)
    b = beta_logit.reshape(8, 256)
    pay, keep, x, l = maps(token_blocks, k, v, g, b)
    got = lax.ppermute(pay, "ctx", [(0, 1), (1, 0)])
    rows = final(pay, keep, got)
    spread = lax.all_to_all(rows.reshape(32, 16, 128), "sess", 0, 0, tiled=True)
    out = reads(token_blocks, q, k, v, g, b, x, l, got)
    place = jnp.arange(32, dtype=jnp.int32)
    owner = jnp.sum(jnp.where(slot_map[None, :] == place[:, None], place[None, :], 0), axis=1)
    back = lax.all_to_all(jnp.take(spread, owner, axis=0, mode="clip"), "sess", 0, 0, tiled=True)
    return out.reshape(1, 256, 8, 128), back.reshape(1, 8, 64, 128)


def solution(mesh):
    from jax.sharding import PartitionSpec as P
    placed = (
        P("sess", "ctx", "head", None), P("sess", "ctx", "head", None), P("sess", "ctx", "head", None),
        P("sess", "head", "ctx"), P("sess", "head", "ctx"), P("sess"), P(),
    )
    return jax.shard_map(
        local, mesh=mesh, in_specs=placed,
        out_specs=(P("sess", "ctx", "head", None), P("sess", "head", "ctx", None)),
        check_vma=False,
    )
```

time: 69.6 us -> 60.4 us (0.87)
  blocking collectives: 24.6 us -> 0 us
  starting transfers between devices: 3.96 us -> 15.9 us
  waiting for transfers between devices: 8.59 us -> 19.7 us
  Pallas kernels: 26.5 us -> 18.9 us
    all_to_all x1 -> x0, blocking collectives: 24.6 us -> none  [local(): spread = lax.all_to_all(rows.reshape(32, 16, 128), 'sess', 0, 0, tiled=True)]
    all_to_all x1 -> x2, starting transfers between devices: 3.87 us -> 15.8 us  [the longest x1 11.6 us: local(): spread = lax.all_to_all(rows.reshape(32, 16, 128), 'sess', 0, 0, tiled=True)]
    all_to_all x1 -> x2, waiting for transfers between devices: 6.69 us -> 17.6 us  [the longest x1 13.1 us: local(): spread = lax.all_to_all(rows.reshape(32, 16, 128), 'sess', 0, 0, tiled=True)]
    pallas_call x1, Pallas kernels: 18.4 us -> 10.3 us  [maps(): pl.pallas_call(maps_kernel, out_shape=[jax.ShapeDtypeStruct((8, 128, 128)...]
    pallas_call x1, Pallas kernels: 5.59 us -> 7.59 us  [reads(): pl.pallas_call(reads_kernel, out_shape=jax.ShapeDtypeStruct((2048, 128),...]
    pallas_call x1 -> x0, Pallas kernels: 1.69 us -> none  [reorder(): pl.pallas_call(reorder_kernel, out_shape=jax.ShapeDtypeStruct(x.shape, x....]
    gather x0 -> x1, local copies, waits for them, and re-layouts: none -> 1.29 us  [local(): jnp.take(spread, owner, axis=0, mode='clip')]
    unnamed x15 -> x21, local copies, waits for them, and re-layouts: 4.1 us -> 2.82 us
  transfers between devices with their start and end apart: 2 -> 3, of which waited for: 2 -> 3; matrix products, arithmetic and copies ran while one was open for 0% -> 0% of each run, Pallas kernels for 8% -> 13%
where the time goes in v2:
time: 60.4 us; the launch traced here: 60 us
  waiting for transfers between devices  19.7 us (33%)
  Pallas kernels  18.9 us (31%)
  starting transfers between devices  15.9 us (26%)
  local copies, waits for them, and re-layouts  4.1 us (7%)
  between operations  1.39 us (2%)
    all_to_all x1, waiting for transfers between devices, local(): spread = lax.all_to_all(rows.reshape(32, 16, 128), 'sess', 0, 0, tiled=True)  13.1 us
    all_to_all x1, starting transfers between devices, local(): spread = lax.all_to_all(rows.reshape(32, 16, 128), 'sess', 0, 0, tiled=True)  11.6 us
    pallas_call x1, Pallas kernels, maps(): pl.pallas_call(maps_kernel, out_shape=[jax.ShapeDtypeStruct((8, 128, 128)...  10.3 us
    pallas_call x1, Pallas kernels, reads(): pl.pallas_call(reads_kernel, out_shape=jax.ShapeDtypeStruct((2048, 128),...  7.59 us
    all_to_all x1, waiting for transfers between devices, local(): lax.all_to_all(jnp.take(spread, owner, axis=0, mode='clip'), 'sess', 0, 0...  4.48 us
    all_to_all x1, starting transfers between devices, local(): lax.all_to_all(jnp.take(spread, owner, axis=0, mode='clip'), 'sess', 0, 0...  4.18 us
    unnamed x21, local copies, waits for them, and re-layouts  2.82 us
    ppermute x1, waiting for transfers between devices, local(): got = lax.ppermute(pay, 'ctx', [(0, 1), (1, 0)])  2.11 us
  transfers between devices with their start and end apart: 3, of which 3 were waited for; matrix products, arithmetic and copies ran while one was open for 0% of the time, Pallas kernels for 13%

profile of v2, /device:TPU:6, one launch (start us, length us, event | category | flops | bytes accessed | tf_op | source)
XLA Modules:
  0.0 60.0 jit_solution(8517155966282158669)
XLA Ops:
  1.3 10.3 %maps.1 = (f32[8,128,128]{2,1,0:T(8,128)}, f32[8,128,128]{2,1,0:T(8,128)}, f32[8,2,128,128]{3,2,1,0:T(8,128)}, f32[8,128,128]{2,1,0:T(8,128)}) custom-call(s32[1]{0:T(128)S(6)} %copy.10.tb_hbm.tb, bf16[1024,128]{1,0:T(8,128)(2,1)} %bitcast.10, bf16[2048,128]{1,0:T(8,128)(2,1)} %bitcast.8, f32[8,256]{1,0:T(8,128)} %bitcast.12, f32[8,256]{1,0:T(8,128)} %bitcast.14), custom_call_target="tpu_custom_call" | custom-call | tf_op jit(solution)/shard_map/maps/pallas_call | solution.py:252
  11.6 0.1 collective-permute-start
  11.7 2.1 %collective-permute-done.m_ref.got_ref = f32[8,128,128]{2,1,0:T(8,128)S(1)} collective-permute-done((f32[8,128,128]{2,1,0:T(8,128)}, f32[8,128,128]{2,1,0:T(8,128)S(1)}, u32[]{:S(2)}, u32[]{:S(2)}) %collective-permute-start) | collective-permute-done | bytes 524320 | tf_op jit(solution)/shard_map/ppermute | solution.py:387
  13.8 0.0 copy-start
  13.8 1.0 %copy-done = f32[8,128,128]{2,1,0:T(8,128)S(1)} copy-done((f32[8,128,128]{2,1,0:T(8,128)S(1)}, f32[8,128,128]{2,1,0:T(8,128)}, u32[]{:S(2)}) %copy-start) | copy-done | bytes 524312
  14.8 0.0 copy-start.1
  14.8 1.0 %copy-done.1 = f32[8,128,128]{2,1,0:T(8,128)S(1)} copy-done((f32[8,128,128]{2,1,0:T(8,128)S(1)}, f32[8,128,128]{2,1,0:T(8,128)}, u32[]{:S(2)}) %copy-start.1) | copy-done | bytes 524312
  15.8 0.0 copy-start.9
  15.8 0.0 copy-start.6
  15.8 0.0 copy-start.8
  15.8 1.0 %final.1 = f32[512,128]{1,0:T(8,128)} custom-call(f32[8,128,128]{2,1,0:T(8,128)S(1)} %copy-done, f32[8,128,128]{2,1,0:T(8,128)S(1)} %copy-done.1, f32[8,128,128]{2,1,0:T(8,128)S(1)} %collective-permute-done.m_ref.got_ref), custom_call_target="tpu_custom_call" | custom-call | tf_op jit(solution)/shard_map/final/pallas_call | solution.py:292
  16.9 0.0 copy-start.7
  16.9 11.6 %all-to-all-start = ((f32[32,16,128]{2,1,0:T(8,128)}), f32[32,16,128]{2,1,0:T(8,128)S(1)}, u32[]{:S(2)}, u32[]{:S(2)}) async-start(f32[32,16,128]{2,1,0:T(8,128)} %bitcast.6), calls=%async_computation | async-start | bytes 524288 | tf_op jit(solution)/shard_map/all_to_all | solution.py:389
  28.5 0.0 copy-done.9
  28.5 0.1 select_reduce_fusion
  28.6 0.0 copy-start.2
  28.6 13.1 %all-to-all-done = f32[32,16,128]{2,1,0:T(8,128)S(1)} async-done(((f32[32,16,128]{2,1,0:T(8,128)}), f32[32,16,128]{2,1,0:T(8,128)S(1)}, u32[]{:S(2)}, u32[]{:S(2)}) %all-to-all-start) | async-done | bytes 262176 | tf_op jit(solution)/shard_map/all_to_all | solution.py:389
  41.7 1.3 %gather_fusion = f32[32,16,128]{2,1,0:T(8,128)} fusion(f32[32,16,128]{2,1,0:T(8,128)S(1)} %all-to-all-done, s32[1024]{0:T(1024)S(1)} %pad_clamp_fusion), kind=kCustom, calls=%fused_computation | custom fusion | bytes 524416 | tf_op jit(solution)/shard_map/jit(_take)/gather | solution.py:393
  43.0 0.0 copy-start.3
  43.0 0.0 copy-start.4
  43.0 0.0 copy-start.5
  43.0 4.2 %all-to-all-start.1 = ((f32[32,16,128]{2,1,0:T(8,128)}), f32[32,16,128]{2,1,0:T(8,128)S(1)}, u32[]{:S(2)}, u32[]{:S(2)}) async-start(f32[32,16,128]{2,1,0:T(8,128)} %gather_fusion), calls=%async_computation.1 | async-start | bytes 524288 | tf_op jit(solution)/shard_map/all_to_all | solution.py:393
  47.2 0.0 copy-done.6
  47.2 0.0 copy-done.8
  47.2 0.0 copy-done.7
  47.2 0.0 copy-done.2
  47.2 0.0 copy-done.3
  47.2 0.0 copy-done.4
  47.3 0.0 copy-done.5
  47.3 7.6 %reads.1 = bf16[2048,128]{1,0:T(8,128)(2,1)} custom-call(s32[1]{0:T(128)S(6)} %copy.10.tb_hbm.tb, bf16[1024,128]{1,0:T(8,128)(2,1)S(1)} %bitcast.16, bf16[1024,128]{1,0:T(8,128)(2,1)S(1)} %bitcast.11, bf16[2048,128]{1,0:T(8,128)(2,1)S(1)} %bitcast.9, f32[8,256]{1,0:T(8,128)S(1)} %bitcast.13, f32[8,256]{1,0:T(8,128)S(1)} %bitcast.15, ...), custom_call_target="tpu_custom_call" | custom-call | flops 1073741824 | bytes 4194304 | tf_op jit(solution)/shard_map/reads/pallas_call | solution.py:365
  54.9 4.5 %all-to-all-done.1 = f32[32,16,128]{2,1,0:T(8,128)S(1)} async-done(((f32[32,16,128]{2,1,0:T(8,128)}), f32[32,16,128]{2,1,0:T(8,128)S(1)}, u32[]{:S(2)}, u32[]{:S(2)}) %all-to-all-start.1) | async-done | bytes 262176 | tf_op jit(solution)/shard_map/all_to_all | solution.py:393
  59.3 0.7 %copy.11 = f32[1,8,64,128]{3,2,1,0:T(8,128)} copy(f32[1,8,64,128]{3,2,1,0:T(8,128)S(1)} %bitcast.17) | data formatting | bytes 524288
  (1 shorter events, 0.0 us)
Async XLA Ops:
  11.6 2.2 %collective-permute-start = (f32[8,128,128]{2,1,0:T(8,128)}, f32[8,128,128]{2,1,0:T(8,128)S(1)}, u32[]{:S(2)}, u32[]{:S(2)}) collective-permute-start(f32[8,128,128]{2,1,0:T(8,128)} %get-tuple-element.8.pay_ref), channel_id=1, source_target_pairs={{0,128},{128,0},{1,129},{129,1},{2,130},{130,2},{3,131},{131,3},{4... | collective-permute-start | bytes 1572872 | tf_op jit(solution)/shard_map/ppermute | solution.py:387
  13.8 1.0 %copy-start = (f32[8,128,128]{2,1,0:T(8,128)S(1)}, f32[8,128,128]{2,1,0:T(8,128)}, u32[]{:S(2)}) copy-start(f32[8,128,128]{2,1,0:T(8,128)} %get-tuple-element.8.pay_ref) | copy-start | bytes 1572868
  14.8 1.0 %copy-start.1 = (f32[8,128,128]{2,1,0:T(8,128)S(1)}, f32[8,128,128]{2,1,0:T(8,128)}, u32[]{:S(2)}) copy-start(f32[8,128,128]{2,1,0:T(8,128)} %get-tuple-element.9.keep_ref) | copy-start | bytes 1572868
  15.8 12.6 %copy-start.9 = (s32[32]{0:T(128)S(1)}, s32[32]{0:T(128)}, u32[]{:S(2)}) copy-start(s32[32]{0:T(128)} %param.13) | copy-start | bytes 388
  15.8 31.4 %copy-start.6 = (f32[8,2,128,128]{3,2,1,0:T(8,128)S(1)}, f32[8,2,128,128]{3,2,1,0:T(8,128)}, u32[]{:S(2)}) copy-start(f32[8,2,128,128]{3,2,1,0:T(8,128)} %get-tuple-element.6.x_ref) | copy-start | bytes 3145732
  15.8 31.4 %copy-start.8 = (bf16[1,256,4,128]{3,2,1,0:T(4,128)(2,1)S(1)}, bf16[1,256,4,128]{3,2,1,0:T(4,128)(2,1)}, u32[]{:S(2)}) copy-start(bf16[1,256,4,128]{3,2,1,0:T(4,128)(2,1)} %param.7) | copy-start | bytes 786436
  16.9 30.4 %copy-start.7 = (f32[8,128,128]{2,1,0:T(8,128)S(1)}, f32[8,128,128]{2,1,0:T(8,128)}, u32[]{:S(2)}) copy-start(f32[8,128,128]{2,1,0:T(8,128)} %get-tuple-element.7.l_ref) | copy-start | bytes 1572868
  16.9 24.8 %all-to-all-start = ((f32[32,16,128]{2,1,0:T(8,128)}), f32[32,16,128]{2,1,0:T(8,128)S(1)}, u32[]{:S(2)}, u32[]{:S(2)}) async-start(f32[32,16,128]{2,1,0:T(8,128)} %bitcast.6), calls=%async_computation | async-start | bytes 524288 | tf_op jit(solution)/shard_map/all_to_all | solution.py:389
  28.6 18.6 %copy-start.2 = (bf16[1,256,8,128]{3,2,1,0:T(8,128)(2,1)S(1)}, bf16[1,256,8,128]{3,2,1,0:T(8,128)(2,1)}, u32[]{:S(2)}) copy-start(bf16[1,256,8,128]{3,2,1,0:T(8,128)(2,1)} %param.9) | copy-start | bytes 1572868
  43.0 4.2 %copy-start.3 = (bf16[1,256,4,128]{3,2,1,0:T(4,128)(2,1)S(1)}, bf16[1,256,4,128]{3,2,1,0:T(4,128)(2,1)}, u32[]{:S(2)}) copy-start(bf16[1,256,4,128]{3,2,1,0:T(4,128)(2,1)} %param.8) | copy-start | bytes 786436
  43.0 4.2 %copy-start.4 = (f32[1,8,256]{2,1,0:T(8,128)S(1)}, f32[1,8,256]{2,1,0:T(8,128)}, u32[]{:S(2)}) copy-start(f32[1,8,256]{2,1,0:T(8,128)} %param.10) | copy-start | bytes 24580
  43.0 4.3 %copy-start.5 = (f32[1,8,256]{2,1,0:T(8,128)S(1)}, f32[1,8,256]{2,1,0:T(8,128)}, u32[]{:S(2)}) copy-start(f32[1,8,256]{2,1,0:T(8,128)} %param.11) | copy-start | bytes 24580
  43.0 16.3 %all-to-all-start.1 = ((f32[32,16,128]{2,1,0:T(8,128)}), f32[32,16,128]{2,1,0:T(8,128)S(1)}, u32[]{:S(2)}, u32[]{:S(2)}) async-start(f32[32,16,128]{2,1,0:T(8,128)} %gather_fusion), calls=%async_computation.1 | async-start | bytes 524288 | tf_op jit(solution)/shard_map/all_to_all | solution.py:393

commit v3 on v2

--- a/solution.py
+++ b/solution.py
@@ -103,24 +103,43 @@
     return -(jnp.maximum(-x, 0.0) + jnp.log1p(jnp.exp(-jnp.abs(x))))
 
 
+def prod(left, right):
+    if MODE == 0:
+        return fold(mm(left, jnp.concatenate([right, right], axis=0)))
+    m = left.shape[0]
+    r = mm(jnp.concatenate([left[:, :128], left[:, 128:]], axis=0), right)
+    return r[:m, :128] + r[:m, 128:] + r[m:, :128]
+
+
+def unpack(p):
+    return p[:, :128].astype(F32) + p[:, 128:].astype(F32)
+
+
+def running_sum(x):
+    r = lax.broadcasted_iota(jnp.int32, (256, 256), 0)
+    c = lax.broadcasted_iota(jnp.int32, (256, 256), 1)
+    tri = jnp.where(r <= c, 1.0, 0.0).astype(BF16)
+    parts = jnp.concatenate([p.astype(F32) for p in split3(x)] + [jnp.zeros((8, 256), F32)], axis=0)
+    y = mm(parts.astype(BF16), tri)
+    return y[:8] + y[8:16] + y[16:24]
+
+
 def spans(left, right):
     ones = jnp.ones((24, 256), F32)
     lhs = jnp.concatenate([p.astype(F32) for p in split3(left)] + [ones, jnp.zeros((80, 256), F32)], axis=0)
-    cols = lhs.T.astype(BF16)
-    rhs = jnp.concatenate([ones.astype(F32)] + [p.astype(F32) for p in split3(-right)] + [jnp.zeros((80, 256), F32)], axis=0)
-    at = lax.broadcasted_iota(jnp.int32, (128, 256), 0) % 8
+    cols = lhs.T.astype(BF16)[:, :64]
+    rhs = jnp.concatenate([ones] + [p.astype(F32) for p in split3(-right)] + [jnp.zeros((16, 256), F32)], axis=0)
+    at = lax.broadcasted_iota(jnp.int32, (64, 256), 0) % 8
     return cols, lambda h: jnp.where(at == h, rhs, 0.0).astype(BF16)
 
 
 def maps_kernel(
-    tb_hbm, k_hbm, v_hbm, g_hbm, b_hbm, pay_ref, keep_ref, x_ref, l21,
-    tb, kr, vr, gr, br, kf, vf, kks, kt, rows, l11, l22, cmp_ref, xc, sems,
+    tb, slot_hbm, k_hbm, v_hbm, g_hbm, b_hbm, pay_ref, keep_ref, x_ref, l21, slot_ref,
+    kr, vr, gr, br, kf, vf, kks, kt, rows, l11, l22, p11, p22, cmp_ref, xc, bb, mid, sems,
 ):
     copies = [
         pltpu.make_async_copy(src, dst, sems.at[i])
-        for i, (src, dst) in enumerate(
-            [(tb_hbm, tb), (k_hbm, kr), (g_hbm, gr), (b_hbm, br), (v_hbm, vr)]
-        )
+        for i, (src, dst) in enumerate([(k_hbm, kr), (g_hbm, gr), (b_hbm, br), (v_hbm, vr), (slot_hbm, slot_ref)])
     ]
     for c in copies:
         c.start()
@@ -130,6 +149,18 @@
     lower = row > col
     eye = row == col
     copies[1].wait()
+    copies[2].wait()
+    edge = tb[0] * 128 - ctx * 256
+    live = lax.broadcasted_iota(jnp.int32, (8, 256), 1) < edge
+    gate = gr[...]
+    steps = -(jnp.maximum(gate, 0.0) + jnp.log1p(jnp.exp(-jnp.abs(gate))))
+    G = running_sum(jnp.where(live, steps, 0.0))
+    lb = log_beta(br[...])
+    last = G[:, 255:256]
+    rows[1] = jnp.where(live, jnp.exp(lb), 0.0)
+    rows[3] = jnp.broadcast_to(jnp.exp(last), (8, 256))
+    early = G + jnp.where(live, lb, -1e4)
+    copies[0].wait()
     kf[...] = kr[...].astype(F32)
     norms = []
     for kh in range(4):
@@ -144,27 +175,22 @@
         s2 = jnp.sum(jnp.where(eye, kk2[:, 128:], 0.0), axis=0, keepdims=True)
         norms.append(jnp.concatenate([s1, s2], axis=1))
     ln = -0.5 * jnp.log(jnp.concatenate([norms[h // 2] for h in range(8)], axis=0) + 1e-06)
-    copies[0].wait()
-    copies[2].wait()
-    copies[3].wait()
-    edge = tb[0] * 128 - ctx * 256
-    live = lax.broadcasted_iota(jnp.int32, (8, 256), 1) < edge
-    G = decay_rows(gr[...], live)
-    a = G + ln + jnp.where(live, log_beta(br[...]), -1e4)
-    last = G[:, 255:256]
+    a = early + ln
     rows[0] = jnp.exp(a)
-    rows[1] = jnp.where(live, jnp.exp(log_beta(br[...])), 0.0)
     rows[2] = jnp.exp(last - G + ln)
-    rows[3] = jnp.broadcast_to(jnp.exp(last), (8, 256))
     cols, right = spans(a, G - ln)
     for h in range(8):
         kh = h // 2
         r = right(h)
         d1 = mm(cols[:128], r[:, :128])
         d2 = mm(cols[128:], r)
-        l11[h] = jnp.where(lower, jnp.exp(d1) * kks[kh, :128, :128], 0.0)
-        l21[h] = jnp.exp(d2[:, :128]) * kks[kh, 128:, :128]
-        l22[h] = jnp.where(lower, jnp.exp(d2[:, 128:]) * kks[kh, 128:, 128:], 0.0)
+        t11 = jnp.where(lower, jnp.exp(d1) * kks[kh, :128, :128], 0.0)
+        t22 = jnp.where(lower, jnp.exp(d2[:, 128:]) * kks[kh, 128:, 128:], 0.0)
+        l11[h] = t11
+        l22[h] = t22
+        p11[h] = pack_left(t11)
+        p22[h] = pack_left(t22)
+        l21[h] = pack_left(jnp.exp(d2[:, :128]) * kks[kh, 128:, :128])
 
     group = lax.broadcasted_iota(jnp.int32, (16, 128), 1) // 16
     for kb in range(16):
@@ -179,6 +205,9 @@
             acc = jnp.where(group == q, t, acc)
         cmp_ref[kb * 16 : kb * 16 + 16, :] = acc
 
+    copies[3].wait()
+    copies[4].wait()
+    vf[...] = vr[...].astype(F32)
     lane = lax.broadcasted_iota(jnp.int32, (16, 128), 1)
     base = (lane // 16) * 16
     xs = [jnp.where(lane % 16 == i, 1.0, 0.0).astype(F32) for i in range(16)]
@@ -190,43 +219,65 @@
             xs[i] = xs[i] - coef * xs[j]
 
     block = row // 16 == col // 16
-    for h in range(8):
-        for part, src in ((0, l11), (1, l22)):
-            x = xc[part * 128 : part * 128 + 128, :]
-            x = jnp.take_along_axis(x, h * 16 + col % 16, axis=1, mode="promise_in_bounds")
-            x_ref[h, part] = jnp.where(block, x, 0.0)
-    halfrow = lax.broadcasted_iota(jnp.int32, (64, 128), 0)
-    halfcol = lax.broadcasted_iota(jnp.int32, (64, 128), 1)
+    if EXPAND == 0:
+        col16, block16 = col[:EG] % 16, [row[i : i + EG] // 16 == col[i : i + EG] // 16 for i in range(0, 128, EG)]
+        for part in range(2):
+            for i in range(0, 128, EG):
+                x = xc[part * 128 + i : part * 128 + i + EG, :]
+                ys = [jnp.take_along_axis(x, h * 16 + col16, axis=1, mode="promise_in_bounds") for h in range(8)]
+                ys = [pack_left(jnp.where(block16[i // EG], y, 0.0)) for y in ys]
+                for h in range(8):
+                    x_ref[h, part, i : i + EG] = ys[h]
+    else:
+        src = lax.broadcasted_iota(jnp.int32, (128, 256), 0)
+        dst = lax.broadcasted_iota(jnp.int32, (128, 256), 1)
+        both = jnp.concatenate(split(xc[...]), axis=0)
+        for p in range(4):
+            pick = jnp.where(src == (2 * p + dst // 128) * 16 + dst % 16, 1.0, 0.0).astype(BF16)
+            r = mm(both, pick)
+            for s in range(2):
+                for part in range(2):
+                    hi = jnp.where(block, r[part * 128 : part * 128 + 128, s * 128 : s * 128 + 128], 0.0)
+                    lo = jnp.where(block, r[256 + part * 128 : 384 + part * 128, s * 128 : s * 128 + 128], 0.0)
+                    x_ref[2 * p + s, part, :, :128] = hi.astype(BF16)
+                    x_ref[2 * p + s, part, :, 128:] = lo.astype(BF16)
+    halfrow = lax.broadcasted_iota(jnp.int32, (64, 256), 0)
+    halfcol = lax.broadcasted_iota(jnp.int32, (64, 256), 1) % 128
+    zero = jnp.zeros((64, 256), BF16)
     for b in (16, 32, 64):
         under = halfcol // b == (halfrow // b) * 2
-        for h in range(8):
-            for part, src in ((0, l11), (1, l22)):
-                x = x_ref[h, part]
-                l = jnp.where(under, picked(src[h], b, 1), 0.0)
-                m = fold(mm(pack_left(l), pack_right(x)))
-                zero = jnp.zeros((64, 128), BF16)
-                mh, ml = split(m)
-                odd = picked(x, b, 1)
-                right_m = twice([woven(zero, mh, b), woven(zero, ml, b)])
-                odd = odd - fold(mm(pack_left(odd), right_m))
-                x_ref[h, part] = woven(picked(x, b, 0), odd, b)
-
-    copies[4].wait()
-    vf[...] = vr[...].astype(F32)
-    for h in range(8):
-        kh = h // 2
-        k = kf[pl.ds(kh, 256, stride=4), :].astype(BF16)
+        pairs = [(h, part, src) for h in range(8) for part, src in ((0, p11), (1, p22))]
+        for h, part, src in pairs:
+            l = jnp.where(under, picked(src[h], b, 1), zero)
+            mid[h, part] = pack_left(prod(l, x_ref[h, part]))
+        for h, part, src in pairs:
+            odd = picked(x_ref[h, part], b, 1)
+            new = pack_left(unpack(odd) - prod(odd, woven(zero, mid[h, part], b)))
+            for i in range(0, 64, b):
+                x_ref[h, part, 2 * i + b : 2 * i + 2 * b] = new[i : i + b]
+
+    for h in range(8):
+        ktz = kt[h // 2] * rows[2, h : h + 1, :]
+        b2 = prod(pack_left(ktz[:, 128:]), x_ref[h, 1])
+        bb[h, :, 128:] = b2
+        l11[h] = ktz[:, :128]
+        p22[h] = pack_left(b2)
+    for h in range(8):
+        p11[h] = pack_left(l11[h] - prod(p22[h], l21[h]))
+    for h in range(8):
+        bb[h, :, :128] = prod(p11[h], x_ref[h, 0])
+    for h in range(8):
+        k = kf[pl.ds((h // 2), 256, stride=4), :].astype(BF16)
+        t = mm(jnp.concatenate(split(bb[h] * rows[0, h : h + 1, :]), axis=0), k)
+        t = jnp.where(eye, rows[3, h : h + 1, :128], 0.0) - (t[:128] + t[128:])
+        l11[h] = t
+        keep_ref[h, :64] = t[64:]
+    for h in range(8):
         v = vf[pl.ds(h, 256, stride=8), :].astype(BF16)
-        ktz = kt[kh] * rows[2, h : h + 1, :]
-        b2 = mm_small(ktz[:, 128:], x_ref[h, 1])
-        b1 = mm_small(ktz[:, :128] - mm_small(b2, l21[h]), x_ref[h, 0])
-        bb = jnp.concatenate([b1, b2], axis=1)
-        t = mm(jnp.concatenate(split(bb * rows[0, h : h + 1, :]), axis=0), k)
-        u = mm(jnp.concatenate(split(bb * rows[1, h : h + 1, :]), axis=0), v)
-        t = jnp.where(eye, rows[3, h : h + 1, :128], 0.0) - (t[:128] + t[128:])
+        u = mm(jnp.concatenate(split(bb[h] * rows[1, h : h + 1, :]), axis=0), v)
         u = u[:128] + u[128:]
-        pay_ref[h] = jnp.where(ctx == 0, u, jnp.concatenate([t[:64], u[:64]], axis=0))
-        keep_ref[h] = jnp.concatenate([t[64:], u[64:]], axis=0)
+        keep_ref[h, 64:] = u[64:]
+        pay_ref[h] = jnp.where(ctx == 0, u, jnp.concatenate([l11[h, :64], u[:64]], axis=0))
 
 
 HEADS_PER_STEP = 4
@@ -244,32 +295,36 @@
     return pl.BlockSpec(memory_space=pltpu.HBM)
 
 
-VL = 60
-
-
-def maps(tb, k, v, g, b):
+VL = 24
+MODE = 0
+EG = 16
+EXPAND = 0
+
+
+def maps(tb, slot_map, k, v, g, b):
     big = lambda *s: pltpu.VMEM(s, F32)
     return pl.pallas_call(
         maps_kernel,
         out_shape=[
-            jax.ShapeDtypeStruct((8, 128, 128), F32),
-            jax.ShapeDtypeStruct((8, 128, 128), F32),
-            jax.ShapeDtypeStruct((8, 2, 128, 128), F32),
-            jax.ShapeDtypeStruct((8, 128, 128), F32),
+            pltpu.VMEM((8, 128, 128), F32),
+            pltpu.VMEM((8, 128, 128), F32),
+            pltpu.VMEM((8, 2, 128, 256), BF16),
+            pltpu.VMEM((8, 128, 256), BF16),
+            pltpu.SMEM((32,), jnp.int32),
         ],
-        in_specs=[hbm()] * 5,
-        out_specs=[vm()] * 4,
+        in_specs=[sm()] + [hbm()] * 5,
+        out_specs=[vm()] * 4 + [sm()],
         scratch_shapes=[
-            pltpu.SMEM((1,), jnp.int32),
             pltpu.VMEM((1024, 128), BF16), pltpu.VMEM((2048, 128), BF16), big(8, 256), big(8, 256),
             big(1024, 128), big(2048, 128), big(4, 256, 256), big(4, 128, 256), big(4, 8, 256),
             big(8, 128, 128), big(8, 128, 128),
-            big(256, 128), big(256, 128),
+            pltpu.VMEM((8, 128, 256), BF16), pltpu.VMEM((8, 128, 256), BF16),
+            big(256, 128), big(256, 128), big(8, 128, 256), pltpu.VMEM((8, 2, 64, 256), BF16),
             pltpu.SemaphoreType.DMA((5,)),
         ],
         compiler_params=pltpu.CompilerParams(vmem_limit_bytes=VL * 2**20),
         name="maps",
-    )(tb, k, v, g, b)
+    )(tb, *[pltpu.with_memory_space_constraint(a, pltpu.HBM) for a in (slot_map, k, v, g, b)])
 
 
 def final_kernel(pay_ref, keep_ref, got_ref, out_ref):
@@ -291,10 +346,10 @@
 def final(pay, keep, got):
     return pl.pallas_call(
         final_kernel,
-        out_shape=jax.ShapeDtypeStruct((512, 128), F32),
+        out_shape=pltpu.VMEM((512, 128), F32),
         in_specs=[vm(), vm(), vm()],
         out_specs=vm(),
-        compiler_params=pltpu.CompilerParams(vmem_limit_bytes=32 * 2**20),
+        compiler_params=pltpu.CompilerParams(vmem_limit_bytes=16 * 2**20),
         name="final",
     )(pay, keep, got)
 
@@ -341,8 +396,8 @@
             mrow = jnp.concatenate(split(m_ref[h] * has), axis=1)
             km = fold(mm(kq, mrow))
             d = bcol[h] * vf[pl.ds(h, 256, stride=8), :] - rcol[h] * km[:256]
-            d1 = mm_small(x_ref[h, 0], d[:128])
-            d2 = mm_small(x_ref[h, 1], d[128:] - mm_small(l_ref[h], d1))
+            d1 = prod(x_ref[h, 0], pack_left(d[:128]))
+            d2 = prod(x_ref[h, 1], pack_left(d[128:] - prod(l_ref[h], pack_left(d1))))
             qm = km[256:] * ecol[h]
             r = right(h)
             e1 = mm(cols[:128], r[:, :128])
@@ -371,10 +426,45 @@
             big(1024, 128), big(1024, 128), big(2048, 128),
             big(8, 256, 128), big(8, 256, 128), big(8, 256, 128), big(2048, 128),
         ],
-        compiler_params=pltpu.CompilerParams(vmem_limit_bytes=40 * 2**20),
+        compiler_params=pltpu.CompilerParams(vmem_limit_bytes=24 * 2**20),
         cost_estimate=pl.CostEstimate(flops=8 * 4 * 2 * 256**3, bytes_accessed=4 * 2**20, transcendentals=0),
         name="reads",
     )(tb, q, k, v, g, b, x, l, m)
+
+
+def reorder_kernel(slot_ref, in_ref, out_ref):
+    for s in range(32):
+        out_ref[slot_ref[s]] = in_ref[s]
+
+
+def reorder(slot_map, x):
+    return pl.pallas_call(
+        reorder_kernel,
+        out_shape=pltpu.VMEM(x.shape, x.dtype),
+        in_specs=[sm(), vm()],
+        out_specs=vm(),
+        name="reorder",
+    )(
+        pltpu.with_memory_space_constraint(slot_map, pltpu.SMEM),
+        pltpu.with_memory_space_constraint(x, pltpu.VMEM),
+    )
+
+
+def place_kernel(in_ref, out_hbm, sem):
+    copy = pltpu.make_async_copy(in_ref, out_hbm, sem)
+    copy.start()
+    copy.wait()
+
+
+def place(x):
+    return pl.pallas_call(
+        place_kernel,
+        out_shape=jax.ShapeDtypeStruct(x.shape, x.dtype),
+        in_specs=[vm()],
+        out_specs=hbm(),
+        scratch_shapes=[pltpu.SemaphoreType.DMA],
+        name="place",
+    )(pltpu.with_memory_space_constraint(x, pltpu.VMEM))
 
 
 def local(queries, keys, values, gate_logit, beta_logit, token_blocks, slot_map):
@@ -383,15 +473,14 @@
     v = values.reshape(2048, 128)
     g = gate_logit.reshape(8, 256)
     b = beta_logit.reshape(8, 256)
-    pay, keep, x, l = maps(token_blocks, k, v, g, b)
+    pay, keep, x, l, slots = maps(token_blocks, slot_map, k, v, g, b)
     got = lax.ppermute(pay, "ctx", [(0, 1), (1, 0)])
     rows = final(pay, keep, got)
     spread = lax.all_to_all(rows.reshape(32, 16, 128), "sess", 0, 0, tiled=True)
     out = reads(token_blocks, q, k, v, g, b, x, l, got)
-    place = jnp.arange(32, dtype=jnp.int32)
-    owner = jnp.sum(jnp.where(slot_map[None, :] == place[:, None], place[None, :], 0), axis=1)
-    back = lax.all_to_all(jnp.take(spread, owner, axis=0, mode="clip"), "sess", 0, 0, tiled=True)
-    return out.reshape(1, 256, 8, 128), back.reshape(1, 8, 64, 128)
+    back = lax.all_to_all(reorder(slots, spread), "sess", 0, 0, tiled=True)
+    back = place(back.reshape(1, 8, 64, 128))
+    return out.reshape(1, 256, 8, 128), back
 
 
 def solution(mesh):

time: 60.4 us -> 52.2 us (0.86)
  blocking collectives: 0 us -> 24.6 us
  waiting for transfers between devices: 19.7 us -> 6.59 us
  starting transfers between devices: 15.9 us -> 4.09 us
  local copies, waits for them, and re-layouts: 4.1 us -> 0.02 us
  Pallas kernels: 18.9 us -> 15.3 us
    all_to_all x0 -> x1, blocking collectives: none -> 24.6 us  [local(): spread = lax.all_to_all(rows.reshape(32, 16, 128), 'sess', 0, 0, tiled=True)]
    all_to_all x2 -> x1, waiting for transfers between devices: 17.6 us -> 4.69 us  [local(): back = lax.all_to_all(reorder(slots, spread), 'sess', 0, 0, tiled=True)]
    all_to_all x2 -> x1, starting transfers between devices: 15.8 us -> 4 us  [local(): back = lax.all_to_all(reorder(slots, spread), 'sess', 0, 0, tiled=True)]
    pallas_call x2 -> x4, Pallas kernels: 11.3 us -> 7.68 us  [the longest x1 5.93 us: maps(): pl.pallas_call(maps_kernel, out_shape=[pltpu.VMEM((8, 128, 128), F32), pl...]
    unnamed x21 -> x10, local copies, waits for them, and re-layouts: 2.82 us -> 0.02 us
    gather x1 -> x0, local copies, waits for them, and re-layouts: 1.29 us -> none  [local(): jnp.take(spread, owner, axis=0, mode='clip')]
  transfers between devices with their start and end apart: 3 -> 2, of which waited for: 3 -> 2; matrix products, arithmetic and copies ran while one was open for 0% -> 0% of each run, Pallas kernels for 13% -> 15%
where the time goes in v3:
time: 52.2 us; the launch traced here: 52 us
  blocking collectives  24.6 us (47%)
  Pallas kernels  15.3 us (29%)
  waiting for transfers between devices  6.59 us (13%)
  starting transfers between devices  4.09 us (8%)
  between operations  1.36 us (3%)
    all_to_all x1, blocking collectives, local(): spread = lax.all_to_all(rows.reshape(32, 16, 128), 'sess', 0, 0, tiled=True)  24.6 us
    pallas_call x1, Pallas kernels, reads(): pl.pallas_call(reads_kernel, out_shape=jax.ShapeDtypeStruct((2048, 128),...  7.58 us
    pallas_call x1, Pallas kernels, maps(): pl.pallas_call(maps_kernel, out_shape=[pltpu.VMEM((8, 128, 128), F32), pl...  5.93 us
    all_to_all x1, waiting for transfers between devices, local(): back = lax.all_to_all(reorder(slots, spread), 'sess', 0, 0, tiled=True)  4.69 us
    all_to_all x1, starting transfers between devices, local(): back = lax.all_to_all(reorder(slots, spread), 'sess', 0, 0, tiled=True)  4 us
    ppermute x1, waiting for transfers between devices, local(): got = lax.ppermute(pay, 'ctx', [(0, 1), (1, 0)])  1.9 us
  transfers between devices with their start and end apart: 2, of which 2 were waited for; matrix products, arithmetic and copies ran while one was open for 0% of the time, Pallas kernels for 15%

profile of v3, /device:TPU:6, one launch (start us, length us, event | category | flops | bytes accessed | tf_op | source)
XLA Modules:
  0.0 52.0 jit_solution(15397000435348932077)
XLA Ops:
  1.3 5.9 %maps.1 = (f32[8,128,128]{2,1,0:T(8,128)S(1)}, f32[8,128,128]{2,1,0:T(8,128)S(1)}, bf16[8,2,128,256]{3,2,1,0:T(8,128)(2,1)S(1)}, bf16[8,128,256]{2,1,0:T(8,128)(2,1)S(1)}, s32[32]{0:T(128)S(4)}) custom-call(s32[1]{0:T(128)S(6)} %copy.9.tb, s32[32]{0:T(128)} %slot_hbm.1, bf16[1024,128]{1,0:T(8,128)(2,1)} %bitcast.12, bf16[2048,128]{1,0:T(8,128)(2,1)} %bitcast.10, ...), custom_call_target="tpu_custom_call" | custom-call | tf_op jit(solution)/shard_map/maps/pallas_call | solution.py:306
  7.2 0.1 collective-permute-start
  7.3 1.9 %collective-permute-done.m_ref.got_ref = f32[8,128,128]{2,1,0:T(8,128)S(1)} collective-permute-done((f32[8,128,128]{2,1,0:T(8,128)S(1)}, f32[8,128,128]{2,1,0:T(8,128)S(1)}, u32[]{:S(2)}, u32[]{:S(2)}) %collective-permute-start) | collective-permute-done | bytes 524320 | tf_op jit(solution)/shard_map/ppermute | solution.py:477
  9.2 0.3 final.1
  9.5 0.0 copy-start.4
  9.5 24.6 %all_to_all.10.in_ref = f32[32,16,128]{2,1,0:T(8,128)S(1)} all-to-all(f32[32,16,128]{2,1,0:T(8,128)S(1)} %bitcast.8), channel_id=1, replica_groups=mesh['ctx'=2,'head'=4,'sess'=32] {'sess'}, dimensions={0} | all-to-all | bytes 524288 | tf_op jit(solution)/shard_map/all_to_all | solution.py:479
  34.2 0.0 copy-start
  34.2 0.7 %reorder.1 = f32[32,16,128]{2,1,0:T(8,128)} custom-call(s32[32]{0:T(128)S(4)} %get-tuple-element.10.slot_ref, f32[32,16,128]{2,1,0:T(8,128)S(1)} %all_to_all.10.in_ref), custom_call_target="tpu_custom_call" | custom-call | tf_op jit(solution)/shard_map/reorder/pallas_call | solution.py:441
  34.9 0.0 copy-start.1
  34.9 0.0 copy-start.2
  34.9 0.0 copy-start.3
  34.9 4.0 %all-to-all-start.1 = ((f32[32,16,128]{2,1,0:T(8,128)}), f32[32,16,128]{2,1,0:T(8,128)S(1)}, u32[]{:S(2)}, u32[]{:S(2)}) async-start(f32[32,16,128]{2,1,0:T(8,128)} %reorder.1), calls=%async_computation.1 | async-start | bytes 524288 | tf_op jit(solution)/shard_map/all_to_all | solution.py:481
  38.9 0.0 copy-done.4
  38.9 0.0 copy-done
  39.0 0.0 copy-done.1
  39.0 0.0 copy-done.2
  39.0 0.0 copy-done.3
  39.0 7.6 %reads.1 = bf16[2048,128]{1,0:T(8,128)(2,1)} custom-call(s32[1]{0:T(128)S(6)} %copy.9.tb, bf16[1024,128]{1,0:T(8,128)(2,1)S(1)} %bitcast.18, bf16[1024,128]{1,0:T(8,128)(2,1)S(1)} %bitcast.13, bf16[2048,128]{1,0:T(8,128)(2,1)S(1)} %bitcast.11, f32[8,256]{1,0:T(8,128)S(1)} %bitcast.15, f32[8,256]{1,0:T(8,128)S(1)} %bitcast.17, ...), custom_call_target="tpu_custom_call" | custom-call | flops 1073741824 | bytes 4194304 | tf_op jit(solution)/shard_map/reads/pallas_call | solution.py:420
  46.6 4.7 %all-to-all-done.1 = f32[32,16,128]{2,1,0:T(8,128)S(1)} async-done(((f32[32,16,128]{2,1,0:T(8,128)}), f32[32,16,128]{2,1,0:T(8,128)S(1)}, u32[]{:S(2)}, u32[]{:S(2)}) %all-to-all-start.1) | async-done | bytes 262176 | tf_op jit(solution)/shard_map/all_to_all | solution.py:481
  51.3 0.7 %place.1 = f32[1,8,64,128]{3,2,1,0:T(8,128)} custom-call(f32[1,8,64,128]{3,2,1,0:T(8,128)S(1)} %bitcast.9), custom_call_target="tpu_custom_call" | custom-call | tf_op jit(solution)/shard_map/place/pallas_call | solution.py:460
Async XLA Ops:
  7.2 2.0 %collective-permute-start = (f32[8,128,128]{2,1,0:T(8,128)S(1)}, f32[8,128,128]{2,1,0:T(8,128)S(1)}, u32[]{:S(2)}, u32[]{:S(2)}) collective-permute-start(f32[8,128,128]{2,1,0:T(8,128)S(1)} %get-tuple-element.9.pay_ref), channel_id=1, source_target_pairs={{0,128},{128,0},{1,129},{129,1},{2,130},{130,2},{3,131},{131,3},{4... | collective-permute-start | bytes 1572872 | tf_op jit(solution)/shard_map/ppermute | solution.py:477
  9.5 29.4 %copy-start.4 = (bf16[1,256,4,128]{3,2,1,0:T(4,128)(2,1)S(1)}, bf16[1,256,4,128]{3,2,1,0:T(4,128)(2,1)}, u32[]{:S(2)}) copy-start(bf16[1,256,4,128]{3,2,1,0:T(4,128)(2,1)} %param.7) | copy-start | bytes 786436
  34.2 4.8 %copy-start = (bf16[1,256,8,128]{3,2,1,0:T(8,128)(2,1)S(1)}, bf16[1,256,8,128]{3,2,1,0:T(8,128)(2,1)}, u32[]{:S(2)}) copy-start(bf16[1,256,8,128]{3,2,1,0:T(8,128)(2,1)} %param.9) | copy-start | bytes 1572868
  34.9 4.0 %copy-start.1 = (bf16[1,256,4,128]{3,2,1,0:T(4,128)(2,1)S(1)}, bf16[1,256,4,128]{3,2,1,0:T(4,128)(2,1)}, u32[]{:S(2)}) copy-start(bf16[1,256,4,128]{3,2,1,0:T(4,128)(2,1)} %param.8) | copy-start | bytes 786436
  34.9 4.0 %copy-start.2 = (f32[1,8,256]{2,1,0:T(8,128)S(1)}, f32[1,8,256]{2,1,0:T(8,128)}, u32[]{:S(2)}) copy-start(f32[1,8,256]{2,1,0:T(8,128)} %param.10) | copy-start | bytes 24580
  34.9 4.1 %copy-start.3 = (f32[1,8,256]{2,1,0:T(8,128)S(1)}, f32[1,8,256]{2,1,0:T(8,128)}, u32[]{:S(2)}) copy-start(f32[1,8,256]{2,1,0:T(8,128)} %param.11) | copy-start | bytes 24580
  34.9 16.3 %all-to-all-start.1 = ((f32[32,16,128]{2,1,0:T(8,128)}), f32[32,16,128]{2,1,0:T(8,128)S(1)}, u32[]{:S(2)}, u32[]{:S(2)}) async-start(f32[32,16,128]{2,1,0:T(8,128)} %reorder.1), calls=%async_computation.1 | async-start | bytes 524288 | tf_op jit(solution)/shard_map/all_to_all | solution.py:481

commit v4 on v3

--- a/solution.py
+++ b/solution.py
@@ -39,12 +39,6 @@
 
 def mm_small(a, b):
     return fold(mm(pack_left(a), pack_right(b)))
-
-
-def mm_wide(a, b):
-    ah, al = split(a)
-    bh, bl = split(b)
-    return mm(jnp.concatenate([ah, al], axis=1), jnp.concatenate([bh, bh], axis=0)) + mm(ah, bl)
 
 
 def decay_rows(gate, live):
@@ -79,17 +73,12 @@
     return hi, mid, lo
 
 
-def mm_tn(a, b):
-    return lax.dot_general(a, b, (((0,), (0,)), ((), ())), preferred_element_type=F32)
-
-
-def twice(pair):
-    row = jnp.concatenate(pair, axis=1)
-    return jnp.concatenate([row, row], axis=0)
-
-
 def picked(x, b, odd):
     return jnp.concatenate([x[i : i + b] for i in range(odd * b, 128, 2 * b)], axis=0)
+
+
+def rows_of(ref, at, b, odd):
+    return jnp.concatenate([ref[at + (slice(i, i + b),)] for i in range(odd * b, 128, 2 * b)], axis=0)
 
 
 def woven(even, odd, b):
@@ -104,11 +93,7 @@
 
 
 def prod(left, right):
-    if MODE == 0:
-        return fold(mm(left, jnp.concatenate([right, right], axis=0)))
-    m = left.shape[0]
-    r = mm(jnp.concatenate([left[:, :128], left[:, 128:]], axis=0), right)
-    return r[:m, :128] + r[:m, 128:] + r[m:, :128]
+    return fold(mm(left, jnp.concatenate([right, right], axis=0)))
 
 
 def unpack(p):
@@ -135,7 +120,7 @@
 
 def maps_kernel(
     tb, slot_hbm, k_hbm, v_hbm, g_hbm, b_hbm, pay_ref, keep_ref, x_ref, l21, slot_ref,
-    kr, vr, gr, br, kf, vf, kks, kt, rows, l11, l22, p11, p22, cmp_ref, xc, bb, mid, sems,
+    kr, vr, gr, br, kf, vf, kks, kt, rows, l11, l22, p11, p22, cmp_ref, xc, sems,
 ):
     copies = [
         pltpu.make_async_copy(src, dst, sems.at[i])
@@ -207,80 +192,93 @@
 
     copies[3].wait()
     copies[4].wait()
-    vf[...] = vr[...].astype(F32)
     lane = lax.broadcasted_iota(jnp.int32, (16, 128), 1)
     base = (lane // 16) * 16
     xs = [jnp.where(lane % 16 == i, 1.0, 0.0).astype(F32) for i in range(16)]
     ls = [cmp_ref[pl.ds(i, 16, stride=16), :] for i in range(16)]
     for j in range(16):
         xc[pl.ds(j, 16, stride=16), :] = xs[j]
+        vf[j * 128 : j * 128 + 128] = vr[j * 128 : j * 128 + 128].astype(F32)
         for i in range(j + 1, 16):
             coef = jnp.take_along_axis(ls[i], base + j, axis=1, mode="promise_in_bounds")
             xs[i] = xs[i] - coef * xs[j]
 
-    block = row // 16 == col // 16
-    if EXPAND == 0:
-        col16, block16 = col[:EG] % 16, [row[i : i + EG] // 16 == col[i : i + EG] // 16 for i in range(0, 128, EG)]
-        for part in range(2):
-            for i in range(0, 128, EG):
-                x = xc[part * 128 + i : part * 128 + i + EG, :]
-                ys = [jnp.take_along_axis(x, h * 16 + col16, axis=1, mode="promise_in_bounds") for h in range(8)]
-                ys = [pack_left(jnp.where(block16[i // EG], y, 0.0)) for y in ys]
-                for h in range(8):
-                    x_ref[h, part, i : i + EG] = ys[h]
-    else:
-        src = lax.broadcasted_iota(jnp.int32, (128, 256), 0)
-        dst = lax.broadcasted_iota(jnp.int32, (128, 256), 1)
-        both = jnp.concatenate(split(xc[...]), axis=0)
-        for p in range(4):
-            pick = jnp.where(src == (2 * p + dst // 128) * 16 + dst % 16, 1.0, 0.0).astype(BF16)
-            r = mm(both, pick)
-            for s in range(2):
-                for part in range(2):
-                    hi = jnp.where(block, r[part * 128 : part * 128 + 128, s * 128 : s * 128 + 128], 0.0)
-                    lo = jnp.where(block, r[256 + part * 128 : 384 + part * 128, s * 128 : s * 128 + 128], 0.0)
-                    x_ref[2 * p + s, part, :, :128] = hi.astype(BF16)
-                    x_ref[2 * p + s, part, :, 128:] = lo.astype(BF16)
+    col16 = col[:16] % 16
+    block16 = [row[i : i + 16] // 16 == col[i : i + 16] // 16 for i in range(0, 128, 16)]
     halfrow = lax.broadcasted_iota(jnp.int32, (64, 256), 0)
     halfcol = lax.broadcasted_iota(jnp.int32, (64, 256), 1) % 128
     zero = jnp.zeros((64, 256), BF16)
-    for b in (16, 32, 64):
-        under = halfcol // b == (halfrow // b) * 2
-        pairs = [(h, part, src) for h in range(8) for part, src in ((0, p11), (1, p22))]
-        for h, part, src in pairs:
-            l = jnp.where(under, picked(src[h], b, 1), zero)
-            mid[h, part] = pack_left(prod(l, x_ref[h, part]))
-        for h, part, src in pairs:
-            odd = picked(x_ref[h, part], b, 1)
-            new = pack_left(unpack(odd) - prod(odd, woven(zero, mid[h, part], b)))
-            for i in range(0, 64, b):
-                x_ref[h, part, 2 * i + b : 2 * i + 2 * b] = new[i : i + b]
-
-    for h in range(8):
+    under = {
+        b: jnp.where(halfcol // b == (halfrow // b) * 2, 1.0, 0.0).astype(BF16) for b in (16, 32, 64)
+    }
+
+    X, MID, TMP, BB = {}, {}, {}, {}
+
+    def expand(h):
+        for part in range(2):
+            tiles = []
+            for i in range(0, 128, 16):
+                x = xc[part * 128 + i : part * 128 + i + 16, :]
+                x = jnp.take_along_axis(x, h * 16 + col16, axis=1, mode="promise_in_bounds")
+                tiles.append(pack_left(jnp.where(block16[i // 16], x, 0.0)))
+            X[h, part] = jnp.concatenate(tiles, axis=0)
+
+    def half_one(b):
+        def step(h):
+            for part, src in ((0, p11), (1, p22)):
+                l = rows_of(src, (h,), b, 1) * under[b]
+                MID[h, part] = pack_left(prod(l, X[h, part]))
+
+        return step
+
+    def half_two(b):
+        def step(h):
+            for part in range(2):
+                x = X[h, part]
+                odd = picked(x, b, 1)
+                new = pack_left(unpack(odd) - prod(odd, woven(zero, MID[h, part], b)))
+                X[h, part] = woven(picked(x, b, 0), new, b)
+                if b == 64:
+                    x_ref[h, part] = X[h, part]
+
+        return step
+
+    def right_half(h):
         ktz = kt[h // 2] * rows[2, h : h + 1, :]
-        b2 = prod(pack_left(ktz[:, 128:]), x_ref[h, 1])
-        bb[h, :, 128:] = b2
-        l11[h] = ktz[:, :128]
-        p22[h] = pack_left(b2)
-    for h in range(8):
-        p11[h] = pack_left(l11[h] - prod(p22[h], l21[h]))
-    for h in range(8):
-        bb[h, :, :128] = prod(p11[h], x_ref[h, 0])
-    for h in range(8):
+        b2 = prod(pack_left(ktz[:, 128:]), X[h, 1])
+        BB[h, 1] = b2
+        TMP[h, 0] = ktz[:, :128]
+        TMP[h, 1] = pack_left(b2)
+
+    def left_rest(h):
+        TMP[h, 2] = pack_left(TMP[h, 0] - prod(TMP[h, 1], l21[h]))
+
+    def left_half(h):
+        BB[h, 0] = prod(TMP[h, 2], X[h, 0])
+
+    def to_map(h):
         k = kf[pl.ds((h // 2), 256, stride=4), :].astype(BF16)
-        t = mm(jnp.concatenate(split(bb[h] * rows[0, h : h + 1, :]), axis=0), k)
+        bb = jnp.concatenate([BB[h, 0], BB[h, 1]], axis=1)
+        t = mm(jnp.concatenate(split(bb * rows[0, h : h + 1, :]), axis=0), k)
         t = jnp.where(eye, rows[3, h : h + 1, :128], 0.0) - (t[:128] + t[128:])
-        l11[h] = t
+        TMP[h, 3] = t[:64]
         keep_ref[h, :64] = t[64:]
-    for h in range(8):
+
+    def to_state(h):
         v = vf[pl.ds(h, 256, stride=8), :].astype(BF16)
-        u = mm(jnp.concatenate(split(bb[h] * rows[1, h : h + 1, :]), axis=0), v)
+        bb = jnp.concatenate([BB[h, 0], BB[h, 1]], axis=1)
+        u = mm(jnp.concatenate(split(bb * rows[1, h : h + 1, :]), axis=0), v)
         u = u[:128] + u[128:]
         keep_ref[h, 64:] = u[64:]
-        pay_ref[h] = jnp.where(ctx == 0, u, jnp.concatenate([l11[h, :64], u[:64]], axis=0))
-
-
-HEADS_PER_STEP = 4
+        pay_ref[h] = jnp.where(ctx == 0, u, jnp.concatenate([TMP[h, 3], u[:64]], axis=0))
+
+    steps = [expand]
+    for b in (16, 32, 64):
+        steps += [half_one(b), half_two(b)]
+    steps += [right_half, left_rest, left_half, to_map, to_state]
+    for step in steps:
+        for h in range(8):
+            step(h)
 
 
 def vm():
@@ -293,12 +291,6 @@
 
 def hbm():
     return pl.BlockSpec(memory_space=pltpu.HBM)
-
-
-VL = 24
-MODE = 0
-EG = 16
-EXPAND = 0
 
 
 def maps(tb, slot_map, k, v, g, b):
@@ -319,10 +311,10 @@
             big(1024, 128), big(2048, 128), big(4, 256, 256), big(4, 128, 256), big(4, 8, 256),
             big(8, 128, 128), big(8, 128, 128),
             pltpu.VMEM((8, 128, 256), BF16), pltpu.VMEM((8, 128, 256), BF16),
-            big(256, 128), big(256, 128), big(8, 128, 256), pltpu.VMEM((8, 2, 64, 256), BF16),
+            big(256, 128), big(256, 128),
             pltpu.SemaphoreType.DMA((5,)),
         ],
-        compiler_params=pltpu.CompilerParams(vmem_limit_bytes=VL * 2**20),
+        compiler_params=pltpu.CompilerParams(vmem_limit_bytes=24 * 2**20),
         name="maps",
     )(tb, *[pltpu.with_memory_space_constraint(a, pltpu.HBM) for a in (slot_map, k, v, g, b)])
 

time: 52.2 us -> 52.1 us (level)
  no operation moved by 1% of the time
where the time goes in v4:
time: 52.1 us; the launch traced here: 51.9 us
  blocking collectives  24.6 us (47%)
  Pallas kernels  15.2 us (29%)
  waiting for transfers between devices  6.59 us (13%)
  starting transfers between devices  4.09 us (8%)
  between operations  1.36 us (3%)
    all_to_all x1, blocking collectives, local(): spread = lax.all_to_all(rows.reshape(32, 16, 128), 'sess', 0, 0, tiled=True)  24.6 us
    pallas_call x1, Pallas kernels, reads(): pl.pallas_call(reads_kernel, out_shape=jax.ShapeDtypeStruct((2048, 128),...  7.58 us
    pallas_call x1, Pallas kernels, maps(): pl.pallas_call(maps_kernel, out_shape=[pltpu.VMEM((8, 128, 128), F32), pl...  5.82 us
    all_to_all x1, waiting for transfers between devices, local(): back = lax.all_to_all(reorder(slots, spread), 'sess', 0, 0, tiled=True)  4.69 us
    all_to_all x1, starting transfers between devices, local(): back = lax.all_to_all(reorder(slots, spread), 'sess', 0, 0, tiled=True)  4 us
    ppermute x1, waiting for transfers between devices, local(): got = lax.ppermute(pay, 'ctx', [(0, 1), (1, 0)])  1.9 us
  transfers between devices with their start and end apart: 2, of which 2 were waited for; matrix products, arithmetic and copies ran while one was open for 0% of the time, Pallas kernels for 15%

profile of v4, /device:TPU:6, one launch (start us, length us, event | category | flops | bytes accessed | tf_op | source)
XLA Modules:
  0.0 51.9 jit_solution(4630486830910600863)
XLA Ops:
  1.3 5.8 %maps.1 = (f32[8,128,128]{2,1,0:T(8,128)S(1)}, f32[8,128,128]{2,1,0:T(8,128)S(1)}, bf16[8,2,128,256]{3,2,1,0:T(8,128)(2,1)S(1)}, bf16[8,128,256]{2,1,0:T(8,128)(2,1)S(1)}, s32[32]{0:T(128)S(4)}) custom-call(s32[1]{0:T(128)S(6)} %copy.9.tb, s32[32]{0:T(128)} %slot_hbm.1, bf16[1024,128]{1,0:T(8,128)(2,1)} %bitcast.12, bf16[2048,128]{1,0:T(8,128)(2,1)} %bitcast.10, ...), custom_call_target="tpu_custom_call" | custom-call | tf_op jit(solution)/shard_map/maps/pallas_call | solution.py:298
  7.1 0.1 collective-permute-start
  7.2 1.9 %collective-permute-done.m_ref.got_ref = f32[8,128,128]{2,1,0:T(8,128)S(1)} collective-permute-done((f32[8,128,128]{2,1,0:T(8,128)S(1)}, f32[8,128,128]{2,1,0:T(8,128)S(1)}, u32[]{:S(2)}, u32[]{:S(2)}) %collective-permute-start) | collective-permute-done | bytes 524320 | tf_op jit(solution)/shard_map/ppermute | solution.py:469
  9.1 0.3 final.1
  9.4 0.0 copy-start.4
  9.4 24.6 %all_to_all.10.in_ref = f32[32,16,128]{2,1,0:T(8,128)S(1)} all-to-all(f32[32,16,128]{2,1,0:T(8,128)S(1)} %bitcast.8), channel_id=1, replica_groups=mesh['ctx'=2,'head'=4,'sess'=32] {'sess'}, dimensions={0} | all-to-all | bytes 524288 | tf_op jit(solution)/shard_map/all_to_all | solution.py:471
  34.1 0.0 copy-start
  34.1 0.7 %reorder.1 = f32[32,16,128]{2,1,0:T(8,128)} custom-call(s32[32]{0:T(128)S(4)} %get-tuple-element.10.slot_ref, f32[32,16,128]{2,1,0:T(8,128)S(1)} %all_to_all.10.in_ref), custom_call_target="tpu_custom_call" | custom-call | tf_op jit(solution)/shard_map/reorder/pallas_call | solution.py:433
  34.8 0.0 copy-start.1
  34.8 0.0 copy-start.2
  34.8 0.0 copy-start.3
  34.8 4.0 %all-to-all-start.1 = ((f32[32,16,128]{2,1,0:T(8,128)}), f32[32,16,128]{2,1,0:T(8,128)S(1)}, u32[]{:S(2)}, u32[]{:S(2)}) async-start(f32[32,16,128]{2,1,0:T(8,128)} %reorder.1), calls=%async_computation.1 | async-start | bytes 524288 | tf_op jit(solution)/shard_map/all_to_all | solution.py:473
  38.8 0.0 copy-done.4
  38.8 0.0 copy-done
  38.8 0.0 copy-done.1
  38.9 0.0 copy-done.2
  38.9 0.0 copy-done.3
  38.9 7.6 %reads.1 = bf16[2048,128]{1,0:T(8,128)(2,1)} custom-call(s32[1]{0:T(128)S(6)} %copy.9.tb, bf16[1024,128]{1,0:T(8,128)(2,1)S(1)} %bitcast.18, bf16[1024,128]{1,0:T(8,128)(2,1)S(1)} %bitcast.13, bf16[2048,128]{1,0:T(8,128)(2,1)S(1)} %bitcast.11, f32[8,256]{1,0:T(8,128)S(1)} %bitcast.15, f32[8,256]{1,0:T(8,128)S(1)} %bitcast.17, ...), custom_call_target="tpu_custom_call" | custom-call | flops 1073741824 | bytes 4194304 | tf_op jit(solution)/shard_map/reads/pallas_call | solution.py:412
  46.5 4.7 %all-to-all-done.1 = f32[32,16,128]{2,1,0:T(8,128)S(1)} async-done(((f32[32,16,128]{2,1,0:T(8,128)}), f32[32,16,128]{2,1,0:T(8,128)S(1)}, u32[]{:S(2)}, u32[]{:S(2)}) %all-to-all-start.1) | async-done | bytes 262176 | tf_op jit(solution)/shard_map/all_to_all | solution.py:473
  51.2 0.7 %place.1 = f32[1,8,64,128]{3,2,1,0:T(8,128)} custom-call(f32[1,8,64,128]{3,2,1,0:T(8,128)S(1)} %bitcast.9), custom_call_target="tpu_custom_call" | custom-call | tf_op jit(solution)/shard_map/place/pallas_call | solution.py:452
Async XLA Ops:
  7.1 2.0 %collective-permute-start = (f32[8,128,128]{2,1,0:T(8,128)S(1)}, f32[8,128,128]{2,1,0:T(8,128)S(1)}, u32[]{:S(2)}, u32[]{:S(2)}) collective-permute-start(f32[8,128,128]{2,1,0:T(8,128)S(1)} %get-tuple-element.9.pay_ref), channel_id=1, source_target_pairs={{0,128},{128,0},{1,129},{129,1},{2,130},{130,2},{3,131},{131,3},{4... | collective-permute-start | bytes 1572872 | tf_op jit(solution)/shard_map/ppermute | solution.py:469
  9.4 29.4 %copy-start.4 = (bf16[1,256,4,128]{3,2,1,0:T(4,128)(2,1)S(1)}, bf16[1,256,4,128]{3,2,1,0:T(4,128)(2,1)}, u32[]{:S(2)}) copy-start(bf16[1,256,4,128]{3,2,1,0:T(4,128)(2,1)} %param.7) | copy-start | bytes 786436
  34.1 4.8 %copy-start = (bf16[1,256,8,128]{3,2,1,0:T(8,128)(2,1)S(1)}, bf16[1,256,8,128]{3,2,1,0:T(8,128)(2,1)}, u32[]{:S(2)}) copy-start(bf16[1,256,8,128]{3,2,1,0:T(8,128)(2,1)} %param.9) | copy-start | bytes 1572868
  34.8 4.0 %copy-start.1 = (bf16[1,256,4,128]{3,2,1,0:T(4,128)(2,1)S(1)}, bf16[1,256,4,128]{3,2,1,0:T(4,128)(2,1)}, u32[]{:S(2)}) copy-start(bf16[1,256,4,128]{3,2,1,0:T(4,128)(2,1)} %param.8) | copy-start | bytes 786436
  34.8 4.0 %copy-start.2 = (f32[1,8,256]{2,1,0:T(8,128)S(1)}, f32[1,8,256]{2,1,0:T(8,128)}, u32[]{:S(2)}) copy-start(f32[1,8,256]{2,1,0:T(8,128)} %param.10) | copy-start | bytes 24580
  34.8 4.1 %copy-start.3 = (f32[1,8,256]{2,1,0:T(8,128)S(1)}, f32[1,8,256]{2,1,0:T(8,128)}, u32[]{:S(2)}) copy-start(f32[1,8,256]{2,1,0:T(8,128)} %param.11) | copy-start | bytes 24580
  34.8 16.3 %all-to-all-start.1 = ((f32[32,16,128]{2,1,0:T(8,128)}), f32[32,16,128]{2,1,0:T(8,128)S(1)}, u32[]{:S(2)}, u32[]{:S(2)}) async-start(f32[32,16,128]{2,1,0:T(8,128)} %reorder.1), calls=%async_computation.1 | async-start | bytes 524288 | tf_op jit(solution)/shard_map/all_to_all | solution.py:473

commit v5 on v3

--- a/solution.py
+++ b/solution.py
@@ -386,13 +386,14 @@
     lower = row >= col
     has = (ctx != 0).astype(F32)
     live1, live2 = edge > 0, edge > 128
-    for kh in range(4):
+    def one(kh, c):
         k = kf[pl.ds(kh, 256, stride=4), :].astype(BF16)
         q = qf[pl.ds(kh, 256, stride=4), :].astype(BF16)
         qk1 = mm_nt(q[:128], k[:128])
         qk2 = mm_nt(q[128:], k)
         kq = jnp.concatenate([k, q], axis=0)
-        for h in (2 * kh, 2 * kh + 1):
+        for j in range(2):
+            h = 2 * kh + j
             mrow = jnp.concatenate(split(m_ref[h] * has), axis=1)
             km = fold(mm(kq, mrow))
             d = bcol[h] * vf[pl.ds(h, 256, stride=8), :] - rcol[h] * km[:256]
@@ -412,6 +413,9 @@
             o1 = jnp.where(live1, o1, 0.0)
             o2 = jnp.where(live2, o2, 0.0)
             of[pl.ds(h, 256, stride=8), :] = jnp.concatenate([o1, o2], axis=0)
+        return c
+
+    lax.fori_loop(0, 4, one, 0)
     o_ref[...] = of[...].astype(BF16)
 
 

time: 52.2 us -> 52.2 us (level)
  waiting for transfers between devices: 6.59 us -> 4.84 us
  Pallas kernels: 15.3 us -> 17 us
    pallas_call x1, Pallas kernels: 7.58 us -> 9.33 us  [reads(): pl.pallas_call(reads_kernel, out_shape=jax.ShapeDtypeStruct((2048, 128),...]
    all_to_all x1, waiting for transfers between devices: 4.69 us -> 2.95 us  [local(): back = lax.all_to_all(reorder(slots, spread), 'sess', 0, 0, tiled=True)]
  transfers between devices with their start and end apart: 2 -> 2, of which waited for: 2 -> 2; matrix products, arithmetic and copies ran while one was open for 0% -> 0% of each run, Pallas kernels for 15% -> 18%
where the time goes in v5:
time: 52.2 us; the launch traced here: 52 us
  blocking collectives  24.6 us (47%)
  Pallas kernels  17 us (33%)
  waiting for transfers between devices  4.84 us (9%)
  starting transfers between devices  4.09 us (8%)
  between operations  1.36 us (3%)
    all_to_all x1, blocking collectives, local(): spread = lax.all_to_all(rows.reshape(32, 16, 128), 'sess', 0, 0, tiled=True)  24.6 us
    pallas_call x1, Pallas kernels, reads(): pl.pallas_call(reads_kernel, out_shape=jax.ShapeDtypeStruct((2048, 128),...  9.33 us
    pallas_call x1, Pallas kernels, maps(): pl.pallas_call(maps_kernel, out_shape=[pltpu.VMEM((8, 128, 128), F32), pl...  5.93 us
    all_to_all x1, starting transfers between devices, local(): back = lax.all_to_all(reorder(slots, spread), 'sess', 0, 0, tiled=True)  4 us
    all_to_all x1, waiting for transfers between devices, local(): back = lax.all_to_all(reorder(slots, spread), 'sess', 0, 0, tiled=True)  2.95 us
    ppermute x1, waiting for transfers between devices, local(): got = lax.ppermute(pay, 'ctx', [(0, 1), (1, 0)])  1.9 us
  transfers between devices with their start and end apart: 2, of which 2 were waited for; matrix products, arithmetic and copies ran while one was open for 0% of the time, Pallas kernels for 18%

profile of v5, /device:TPU:6, one launch (start us, length us, event | category | flops | bytes accessed | tf_op | source)
XLA Modules:
  0.0 52.0 jit_solution(14535770836377149503)
XLA Ops:
  1.3 5.9 %maps.1 = (f32[8,128,128]{2,1,0:T(8,128)S(1)}, f32[8,128,128]{2,1,0:T(8,128)S(1)}, bf16[8,2,128,256]{3,2,1,0:T(8,128)(2,1)S(1)}, bf16[8,128,256]{2,1,0:T(8,128)(2,1)S(1)}, s32[32]{0:T(128)S(4)}) custom-call(s32[1]{0:T(128)S(6)} %copy.9.tb, s32[32]{0:T(128)} %slot_hbm.1, bf16[1024,128]{1,0:T(8,128)(2,1)} %bitcast.12, bf16[2048,128]{1,0:T(8,128)(2,1)} %bitcast.10, ...), custom_call_target="tpu_custom_call" | custom-call | tf_op jit(solution)/shard_map/maps/pallas_call | solution.py:306
  7.2 0.1 collective-permute-start
  7.3 1.9 %collective-permute-done.m_ref.got_ref = f32[8,128,128]{2,1,0:T(8,128)S(1)} collective-permute-done((f32[8,128,128]{2,1,0:T(8,128)S(1)}, f32[8,128,128]{2,1,0:T(8,128)S(1)}, u32[]{:S(2)}, u32[]{:S(2)}) %collective-permute-start) | collective-permute-done | bytes 524320 | tf_op jit(solution)/shard_map/ppermute | solution.py:481
  9.2 0.3 final.1
  9.5 0.0 copy-start.4
  9.5 24.6 %all_to_all.10.in_ref = f32[32,16,128]{2,1,0:T(8,128)S(1)} all-to-all(f32[32,16,128]{2,1,0:T(8,128)S(1)} %bitcast.8), channel_id=1, replica_groups=mesh['ctx'=2,'head'=4,'sess'=32] {'sess'}, dimensions={0} | all-to-all | bytes 524288 | tf_op jit(solution)/shard_map/all_to_all | solution.py:483
  34.2 0.0 copy-start
  34.2 0.7 %reorder.1 = f32[32,16,128]{2,1,0:T(8,128)} custom-call(s32[32]{0:T(128)S(4)} %get-tuple-element.10.slot_ref, f32[32,16,128]{2,1,0:T(8,128)S(1)} %all_to_all.10.in_ref), custom_call_target="tpu_custom_call" | custom-call | tf_op jit(solution)/shard_map/reorder/pallas_call | solution.py:445
  34.9 0.0 copy-start.1
  34.9 0.0 copy-start.2
  34.9 0.0 copy-start.3
  34.9 4.0 %all-to-all-start.1 = ((f32[32,16,128]{2,1,0:T(8,128)}), f32[32,16,128]{2,1,0:T(8,128)S(1)}, u32[]{:S(2)}, u32[]{:S(2)}) async-start(f32[32,16,128]{2,1,0:T(8,128)} %reorder.1), calls=%async_computation.1 | async-start | bytes 524288 | tf_op jit(solution)/shard_map/all_to_all | solution.py:485
  38.9 0.0 copy-done.4
  38.9 0.0 copy-done
  39.0 0.0 copy-done.1
  39.0 0.0 copy-done.2
  39.0 0.0 copy-done.3
  39.0 9.3 %reads.1 = bf16[2048,128]{1,0:T(8,128)(2,1)} custom-call(s32[1]{0:T(128)S(6)} %copy.9.tb, bf16[1024,128]{1,0:T(8,128)(2,1)S(1)} %bitcast.18, bf16[1024,128]{1,0:T(8,128)(2,1)S(1)} %bitcast.13, bf16[2048,128]{1,0:T(8,128)(2,1)S(1)} %bitcast.11, f32[8,256]{1,0:T(8,128)S(1)} %bitcast.15, f32[8,256]{1,0:T(8,128)S(1)} %bitcast.17, ...), custom_call_target="tpu_custom_call" | custom-call | flops 1073741824 | bytes 4194304 | tf_op jit(solution)/shard_map/reads/pallas_call | solution.py:424
  48.3 2.9 %all-to-all-done.1 = f32[32,16,128]{2,1,0:T(8,128)S(1)} async-done(((f32[32,16,128]{2,1,0:T(8,128)}), f32[32,16,128]{2,1,0:T(8,128)S(1)}, u32[]{:S(2)}, u32[]{:S(2)}) %all-to-all-start.1) | async-done | bytes 262176 | tf_op jit(solution)/shard_map/all_to_all | solution.py:485
  51.3 0.7 %place.1 = f32[1,8,64,128]{3,2,1,0:T(8,128)} custom-call(f32[1,8,64,128]{3,2,1,0:T(8,128)S(1)} %bitcast.9), custom_call_target="tpu_custom_call" | custom-call | tf_op jit(solution)/shard_map/place/pallas_call | solution.py:464
Async XLA Ops:
  7.2 2.0 %collective-permute-start = (f32[8,128,128]{2,1,0:T(8,128)S(1)}, f32[8,128,128]{2,1,0:T(8,128)S(1)}, u32[]{:S(2)}, u32[]{:S(2)}) collective-permute-start(f32[8,128,128]{2,1,0:T(8,128)S(1)} %get-tuple-element.9.pay_ref), channel_id=1, source_target_pairs={{0,128},{128,0},{1,129},{129,1},{2,130},{130,2},{3,131},{131,3},{4... | collective-permute-start | bytes 1572872 | tf_op jit(solution)/shard_map/ppermute | solution.py:481
  9.5 29.4 %copy-start.4 = (bf16[1,256,4,128]{3,2,1,0:T(4,128)(2,1)S(1)}, bf16[1,256,4,128]{3,2,1,0:T(4,128)(2,1)}, u32[]{:S(2)}) copy-start(bf16[1,256,4,128]{3,2,1,0:T(4,128)(2,1)} %param.7) | copy-start | bytes 786436
  34.2 4.8 %copy-start = (bf16[1,256,8,128]{3,2,1,0:T(8,128)(2,1)S(1)}, bf16[1,256,8,128]{3,2,1,0:T(8,128)(2,1)}, u32[]{:S(2)}) copy-start(bf16[1,256,8,128]{3,2,1,0:T(8,128)(2,1)} %param.9) | copy-start | bytes 1572868
  34.9 4.0 %copy-start.1 = (bf16[1,256,4,128]{3,2,1,0:T(4,128)(2,1)S(1)}, bf16[1,256,4,128]{3,2,1,0:T(4,128)(2,1)}, u32[]{:S(2)}) copy-start(bf16[1,256,4,128]{3,2,1,0:T(4,128)(2,1)} %param.8) | copy-start | bytes 786436
  34.9 4.0 %copy-start.2 = (f32[1,8,256]{2,1,0:T(8,128)S(1)}, f32[1,8,256]{2,1,0:T(8,128)}, u32[]{:S(2)}) copy-start(f32[1,8,256]{2,1,0:T(8,128)} %param.10) | copy-start | bytes 24580
  34.9 4.1 %copy-start.3 = (f32[1,8,256]{2,1,0:T(8,128)S(1)}, f32[1,8,256]{2,1,0:T(8,128)}, u32[]{:S(2)}) copy-start(f32[1,8,256]{2,1,0:T(8,128)} %param.11) | copy-start | bytes 24580
  34.9 16.3 %all-to-all-start.1 = ((f32[32,16,128]{2,1,0:T(8,128)}), f32[32,16,128]{2,1,0:T(8,128)S(1)}, u32[]{:S(2)}, u32[]{:S(2)}) async-start(f32[32,16,128]{2,1,0:T(8,128)} %reorder.1), calls=%async_computation.1 | async-start | bytes 524288 | tf_op jit(solution)/shard_map/all_to_all | solution.py:485

commit v6 on v4

--- a/solution.py
+++ b/solution.py
@@ -126,8 +126,8 @@
         pltpu.make_async_copy(src, dst, sems.at[i])
         for i, (src, dst) in enumerate([(k_hbm, kr), (g_hbm, gr), (b_hbm, br), (v_hbm, vr), (slot_hbm, slot_ref)])
     ]
-    for c in copies:
-        c.start()
+    for i in (1, 2, 0, 4, 3):
+        copies[i].start()
     ctx = lax.axis_index("ctx")
     row = lax.broadcasted_iota(jnp.int32, (128, 128), 0)
     col = lax.broadcasted_iota(jnp.int32, (128, 128), 1)

time: 52.1 us -> 52.1 us (level)
  no operation moved by 1% of the time
where the time goes in v6:
time: 52.1 us; the launch traced here: 51.8 us
  blocking collectives  24.6 us (47%)
  Pallas kernels  15.1 us (29%)
  waiting for transfers between devices  6.59 us (13%)
  starting transfers between devices  4.09 us (8%)
  between operations  1.36 us (3%)
    all_to_all x1, blocking collectives, local(): spread = lax.all_to_all(rows.reshape(32, 16, 128), 'sess', 0, 0, tiled=True)  24.6 us
    pallas_call x1, Pallas kernels, reads(): pl.pallas_call(reads_kernel, out_shape=jax.ShapeDtypeStruct((2048, 128),...  7.58 us
    pallas_call x1, Pallas kernels, maps(): pl.pallas_call(maps_kernel, out_shape=[pltpu.VMEM((8, 128, 128), F32), pl...  5.79 us
    all_to_all x1, waiting for transfers between devices, local(): back = lax.all_to_all(reorder(slots, spread), 'sess', 0, 0, tiled=True)  4.69 us
    all_to_all x1, starting transfers between devices, local(): back = lax.all_to_all(reorder(slots, spread), 'sess', 0, 0, tiled=True)  4 us
    ppermute x1, waiting for transfers between devices, local(): got = lax.ppermute(pay, 'ctx', [(0, 1), (1, 0)])  1.9 us
  transfers between devices with their start and end apart: 2, of which 2 were waited for; matrix products, arithmetic and copies ran while one was open for 0% of the time, Pallas kernels for 15%

profile of v6, /device:TPU:6, one launch (start us, length us, event | category | flops | bytes accessed | tf_op | source)
XLA Modules:
  0.0 51.8 jit_solution(15793731042895962856)
XLA Ops:
  1.3 5.8 %maps.1 = (f32[8,128,128]{2,1,0:T(8,128)S(1)}, f32[8,128,128]{2,1,0:T(8,128)S(1)}, bf16[8,2,128,256]{3,2,1,0:T(8,128)(2,1)S(1)}, bf16[8,128,256]{2,1,0:T(8,128)(2,1)S(1)}, s32[32]{0:T(128)S(4)}) custom-call(s32[1]{0:T(128)S(6)} %copy.9.tb, s32[32]{0:T(128)} %slot_hbm.1, bf16[1024,128]{1,0:T(8,128)(2,1)} %bitcast.12, bf16[2048,128]{1,0:T(8,128)(2,1)} %bitcast.10, ...), custom_call_target="tpu_custom_call" | custom-call | tf_op jit(solution)/shard_map/maps/pallas_call | solution.py:298
  7.1 0.1 collective-permute-start
  7.2 1.9 %collective-permute-done.m_ref.got_ref = f32[8,128,128]{2,1,0:T(8,128)S(1)} collective-permute-done((f32[8,128,128]{2,1,0:T(8,128)S(1)}, f32[8,128,128]{2,1,0:T(8,128)S(1)}, u32[]{:S(2)}, u32[]{:S(2)}) %collective-permute-start) | collective-permute-done | bytes 524320 | tf_op jit(solution)/shard_map/ppermute | solution.py:469
  9.1 0.3 final.1
  9.4 0.0 copy-start.4
  9.4 24.6 %all_to_all.10.in_ref = f32[32,16,128]{2,1,0:T(8,128)S(1)} all-to-all(f32[32,16,128]{2,1,0:T(8,128)S(1)} %bitcast.8), channel_id=1, replica_groups=mesh['ctx'=2,'head'=4,'sess'=32] {'sess'}, dimensions={0} | all-to-all | bytes 524288 | tf_op jit(solution)/shard_map/all_to_all | solution.py:471
  34.0 0.0 copy-start
  34.0 0.7 %reorder.1 = f32[32,16,128]{2,1,0:T(8,128)} custom-call(s32[32]{0:T(128)S(4)} %get-tuple-element.10.slot_ref, f32[32,16,128]{2,1,0:T(8,128)S(1)} %all_to_all.10.in_ref), custom_call_target="tpu_custom_call" | custom-call | tf_op jit(solution)/shard_map/reorder/pallas_call | solution.py:433
  34.8 0.0 copy-start.1
  34.8 0.0 copy-start.2
  34.8 0.0 copy-start.3
  34.8 4.0 %all-to-all-start.1 = ((f32[32,16,128]{2,1,0:T(8,128)}), f32[32,16,128]{2,1,0:T(8,128)S(1)}, u32[]{:S(2)}, u32[]{:S(2)}) async-start(f32[32,16,128]{2,1,0:T(8,128)} %reorder.1), calls=%async_computation.1 | async-start | bytes 524288 | tf_op jit(solution)/shard_map/all_to_all | solution.py:473
  38.8 0.0 copy-done.4
  38.8 0.0 copy-done
  38.8 0.0 copy-done.1
  38.8 0.0 copy-done.2
  38.8 0.0 copy-done.3
  38.8 7.6 %reads.1 = bf16[2048,128]{1,0:T(8,128)(2,1)} custom-call(s32[1]{0:T(128)S(6)} %copy.9.tb, bf16[1024,128]{1,0:T(8,128)(2,1)S(1)} %bitcast.18, bf16[1024,128]{1,0:T(8,128)(2,1)S(1)} %bitcast.13, bf16[2048,128]{1,0:T(8,128)(2,1)S(1)} %bitcast.11, f32[8,256]{1,0:T(8,128)S(1)} %bitcast.15, f32[8,256]{1,0:T(8,128)S(1)} %bitcast.17, ...), custom_call_target="tpu_custom_call" | custom-call | flops 1073741824 | bytes 4194304 | tf_op jit(solution)/shard_map/reads/pallas_call | solution.py:412
  46.4 4.7 %all-to-all-done.1 = f32[32,16,128]{2,1,0:T(8,128)S(1)} async-done(((f32[32,16,128]{2,1,0:T(8,128)}), f32[32,16,128]{2,1,0:T(8,128)S(1)}, u32[]{:S(2)}, u32[]{:S(2)}) %all-to-all-start.1) | async-done | bytes 262176 | tf_op jit(solution)/shard_map/all_to_all | solution.py:473
  51.1 0.7 %place.1 = f32[1,8,64,128]{3,2,1,0:T(8,128)} custom-call(f32[1,8,64,128]{3,2,1,0:T(8,128)S(1)} %bitcast.9), custom_call_target="tpu_custom_call" | custom-call | tf_op jit(solution)/shard_map/place/pallas_call | solution.py:452
Async XLA Ops:
  7.1 2.0 %collective-permute-start = (f32[8,128,128]{2,1,0:T(8,128)S(1)}, f32[8,128,128]{2,1,0:T(8,128)S(1)}, u32[]{:S(2)}, u32[]{:S(2)}) collective-permute-start(f32[8,128,128]{2,1,0:T(8,128)S(1)} %get-tuple-element.9.pay_ref), channel_id=1, source_target_pairs={{0,128},{128,0},{1,129},{129,1},{2,130},{130,2},{3,131},{131,3},{4... | collective-permute-start | bytes 1572872 | tf_op jit(solution)/shard_map/ppermute | solution.py:469
  9.4 29.4 %copy-start.4 = (bf16[1,256,4,128]{3,2,1,0:T(4,128)(2,1)S(1)}, bf16[1,256,4,128]{3,2,1,0:T(4,128)(2,1)}, u32[]{:S(2)}) copy-start(bf16[1,256,4,128]{3,2,1,0:T(4,128)(2,1)} %param.7) | copy-start | bytes 786436
  34.0 4.8 %copy-start = (bf16[1,256,8,128]{3,2,1,0:T(8,128)(2,1)S(1)}, bf16[1,256,8,128]{3,2,1,0:T(8,128)(2,1)}, u32[]{:S(2)}) copy-start(bf16[1,256,8,128]{3,2,1,0:T(8,128)(2,1)} %param.9) | copy-start | bytes 1572868
  34.8 4.0 %copy-start.1 = (bf16[1,256,4,128]{3,2,1,0:T(4,128)(2,1)S(1)}, bf16[1,256,4,128]{3,2,1,0:T(4,128)(2,1)}, u32[]{:S(2)}) copy-start(bf16[1,256,4,128]{3,2,1,0:T(4,128)(2,1)} %param.8) | copy-start | bytes 786436
  34.8 4.0 %copy-start.2 = (f32[1,8,256]{2,1,0:T(8,128)S(1)}, f32[1,8,256]{2,1,0:T(8,128)}, u32[]{:S(2)}) copy-start(f32[1,8,256]{2,1,0:T(8,128)} %param.10) | copy-start | bytes 24580
  34.8 4.1 %copy-start.3 = (f32[1,8,256]{2,1,0:T(8,128)S(1)}, f32[1,8,256]{2,1,0:T(8,128)}, u32[]{:S(2)}) copy-start(f32[1,8,256]{2,1,0:T(8,128)} %param.11) | copy-start | bytes 24580
  34.8 16.3 %all-to-all-start.1 = ((f32[32,16,128]{2,1,0:T(8,128)}), f32[32,16,128]{2,1,0:T(8,128)S(1)}, u32[]{:S(2)}, u32[]{:S(2)}) async-start(f32[32,16,128]{2,1,0:T(8,128)} %reorder.1), calls=%async_computation.1 | async-start | bytes 524288 | tf_op jit(solution)/shard_map/all_to_all | solution.py:473

commit v7 on v6

--- a/solution.py
+++ b/solution.py
@@ -378,13 +378,14 @@
     lower = row >= col
     has = (ctx != 0).astype(F32)
     live1, live2 = edge > 0, edge > 128
-    for kh in range(4):
+    def one(kh, c):
         k = kf[pl.ds(kh, 256, stride=4), :].astype(BF16)
         q = qf[pl.ds(kh, 256, stride=4), :].astype(BF16)
         qk1 = mm_nt(q[:128], k[:128])
         qk2 = mm_nt(q[128:], k)
         kq = jnp.concatenate([k, q], axis=0)
-        for h in (2 * kh, 2 * kh + 1):
+        for j in range(2):
+            h = 2 * kh + j
             mrow = jnp.concatenate(split(m_ref[h] * has), axis=1)
             km = fold(mm(kq, mrow))
             d = bcol[h] * vf[pl.ds(h, 256, stride=8), :] - rcol[h] * km[:256]
@@ -404,6 +405,9 @@
             o1 = jnp.where(live1, o1, 0.0)
             o2 = jnp.where(live2, o2, 0.0)
             of[pl.ds(h, 256, stride=8), :] = jnp.concatenate([o1, o2], axis=0)
+        return c
+
+    lax.fori_loop(0, 4, one, 0)
     o_ref[...] = of[...].astype(BF16)
 
 

time: 52.1 us -> 52.1 us (level)
  Pallas kernels: 15.1 us -> 16.9 us
  waiting for transfers between devices: 6.59 us -> 4.84 us
    pallas_call x1, Pallas kernels: 7.58 us -> 9.33 us  [reads(): pl.pallas_call(reads_kernel, out_shape=jax.ShapeDtypeStruct((2048, 128),...]
    all_to_all x1, waiting for transfers between devices: 4.69 us -> 2.94 us  [local(): back = lax.all_to_all(reorder(slots, spread), 'sess', 0, 0, tiled=True)]
  transfers between devices with their start and end apart: 2 -> 2, of which waited for: 2 -> 2; matrix products, arithmetic and copies ran while one was open for 0% -> 0% of each run, Pallas kernels for 15% -> 18%
where the time goes in v7:
time: 52.1 us; the launch traced here: 51.8 us
  blocking collectives  24.6 us (47%)
  Pallas kernels  16.9 us (32%)
  waiting for transfers between devices  4.84 us (9%)
  starting transfers between devices  4.09 us (8%)
  between operations  1.36 us (3%)
    all_to_all x1, blocking collectives, local(): spread = lax.all_to_all(rows.reshape(32, 16, 128), 'sess', 0, 0, tiled=True)  24.6 us
    pallas_call x1, Pallas kernels, reads(): pl.pallas_call(reads_kernel, out_shape=jax.ShapeDtypeStruct((2048, 128),...  9.33 us
    pallas_call x1, Pallas kernels, maps(): pl.pallas_call(maps_kernel, out_shape=[pltpu.VMEM((8, 128, 128), F32), pl...  5.79 us
    all_to_all x1, starting transfers between devices, local(): back = lax.all_to_all(reorder(slots, spread), 'sess', 0, 0, tiled=True)  4 us
    all_to_all x1, waiting for transfers between devices, local(): back = lax.all_to_all(reorder(slots, spread), 'sess', 0, 0, tiled=True)  2.94 us
    ppermute x1, waiting for transfers between devices, local(): got = lax.ppermute(pay, 'ctx', [(0, 1), (1, 0)])  1.9 us
  transfers between devices with their start and end apart: 2, of which 2 were waited for; matrix products, arithmetic and copies ran while one was open for 0% of the time, Pallas kernels for 18%

profile of v7, /device:TPU:6, one launch (start us, length us, event | category | flops | bytes accessed | tf_op | source)
XLA Modules:
  0.0 51.8 jit_solution(14728235606074182138)
XLA Ops:
  1.3 5.8 %maps.1 = (f32[8,128,128]{2,1,0:T(8,128)S(1)}, f32[8,128,128]{2,1,0:T(8,128)S(1)}, bf16[8,2,128,256]{3,2,1,0:T(8,128)(2,1)S(1)}, bf16[8,128,256]{2,1,0:T(8,128)(2,1)S(1)}, s32[32]{0:T(128)S(4)}) custom-call(s32[1]{0:T(128)S(6)} %copy.9.tb, s32[32]{0:T(128)} %slot_hbm.1, bf16[1024,128]{1,0:T(8,128)(2,1)} %bitcast.12, bf16[2048,128]{1,0:T(8,128)(2,1)} %bitcast.10, ...), custom_call_target="tpu_custom_call" | custom-call | tf_op jit(solution)/shard_map/maps/pallas_call | solution.py:298
  7.1 0.1 collective-permute-start
  7.2 1.9 %collective-permute-done.m_ref.got_ref = f32[8,128,128]{2,1,0:T(8,128)S(1)} collective-permute-done((f32[8,128,128]{2,1,0:T(8,128)S(1)}, f32[8,128,128]{2,1,0:T(8,128)S(1)}, u32[]{:S(2)}, u32[]{:S(2)}) %collective-permute-start) | collective-permute-done | bytes 524320 | tf_op jit(solution)/shard_map/ppermute | solution.py:473
  9.1 0.3 final.1
  9.4 0.0 copy-start.4
  9.4 24.6 %all_to_all.10.in_ref = f32[32,16,128]{2,1,0:T(8,128)S(1)} all-to-all(f32[32,16,128]{2,1,0:T(8,128)S(1)} %bitcast.8), channel_id=1, replica_groups=mesh['ctx'=2,'head'=4,'sess'=32] {'sess'}, dimensions={0} | all-to-all | bytes 524288 | tf_op jit(solution)/shard_map/all_to_all | solution.py:475
  34.0 0.0 copy-start
  34.0 0.7 %reorder.1 = f32[32,16,128]{2,1,0:T(8,128)} custom-call(s32[32]{0:T(128)S(4)} %get-tuple-element.10.slot_ref, f32[32,16,128]{2,1,0:T(8,128)S(1)} %all_to_all.10.in_ref), custom_call_target="tpu_custom_call" | custom-call | tf_op jit(solution)/shard_map/reorder/pallas_call | solution.py:437
  34.8 0.0 copy-start.1
  34.8 0.0 copy-start.2
  34.8 0.0 copy-start.3
  34.8 4.0 %all-to-all-start.1 = ((f32[32,16,128]{2,1,0:T(8,128)}), f32[32,16,128]{2,1,0:T(8,128)S(1)}, u32[]{:S(2)}, u32[]{:S(2)}) async-start(f32[32,16,128]{2,1,0:T(8,128)} %reorder.1), calls=%async_computation.1 | async-start | bytes 524288 | tf_op jit(solution)/shard_map/all_to_all | solution.py:477
  38.8 0.0 copy-done.4
  38.8 0.0 copy-done
  38.8 0.0 copy-done.1
  38.8 0.0 copy-done.2
  38.8 0.0 copy-done.3
  38.8 9.3 %reads.1 = bf16[2048,128]{1,0:T(8,128)(2,1)} custom-call(s32[1]{0:T(128)S(6)} %copy.9.tb, bf16[1024,128]{1,0:T(8,128)(2,1)S(1)} %bitcast.18, bf16[1024,128]{1,0:T(8,128)(2,1)S(1)} %bitcast.13, bf16[2048,128]{1,0:T(8,128)(2,1)S(1)} %bitcast.11, f32[8,256]{1,0:T(8,128)S(1)} %bitcast.15, f32[8,256]{1,0:T(8,128)S(1)} %bitcast.17, ...), custom_call_target="tpu_custom_call" | custom-call | flops 1073741824 | bytes 4194304 | tf_op jit(solution)/shard_map/reads/pallas_call | solution.py:416
  48.2 2.9 %all-to-all-done.1 = f32[32,16,128]{2,1,0:T(8,128)S(1)} async-done(((f32[32,16,128]{2,1,0:T(8,128)}), f32[32,16,128]{2,1,0:T(8,128)S(1)}, u32[]{:S(2)}, u32[]{:S(2)}) %all-to-all-start.1) | async-done | bytes 262176 | tf_op jit(solution)/shard_map/all_to_all | solution.py:477
  51.1 0.7 %place.1 = f32[1,8,64,128]{3,2,1,0:T(8,128)} custom-call(f32[1,8,64,128]{3,2,1,0:T(8,128)S(1)} %bitcast.9), custom_call_target="tpu_custom_call" | custom-call | tf_op jit(solution)/shard_map/place/pallas_call | solution.py:456
Async XLA Ops:
  7.1 2.0 %collective-permute-start = (f32[8,128,128]{2,1,0:T(8,128)S(1)}, f32[8,128,128]{2,1,0:T(8,128)S(1)}, u32[]{:S(2)}, u32[]{:S(2)}) collective-permute-start(f32[8,128,128]{2,1,0:T(8,128)S(1)} %get-tuple-element.9.pay_ref), channel_id=1, source_target_pairs={{0,128},{128,0},{1,129},{129,1},{2,130},{130,2},{3,131},{131,3},{4... | collective-permute-start | bytes 1572872 | tf_op jit(solution)/shard_map/ppermute | solution.py:473
  9.4 29.4 %copy-start.4 = (bf16[1,256,4,128]{3,2,1,0:T(4,128)(2,1)S(1)}, bf16[1,256,4,128]{3,2,1,0:T(4,128)(2,1)}, u32[]{:S(2)}) copy-start(bf16[1,256,4,128]{3,2,1,0:T(4,128)(2,1)} %param.7) | copy-start | bytes 786436
  34.0 4.8 %copy-start = (bf16[1,256,8,128]{3,2,1,0:T(8,128)(2,1)S(1)}, bf16[1,256,8,128]{3,2,1,0:T(8,128)(2,1)}, u32[]{:S(2)}) copy-start(bf16[1,256,8,128]{3,2,1,0:T(8,128)(2,1)} %param.9) | copy-start | bytes 1572868
  34.8 4.0 %copy-start.1 = (bf16[1,256,4,128]{3,2,1,0:T(4,128)(2,1)S(1)}, bf16[1,256,4,128]{3,2,1,0:T(4,128)(2,1)}, u32[]{:S(2)}) copy-start(bf16[1,256,4,128]{3,2,1,0:T(4,128)(2,1)} %param.8) | copy-start | bytes 786436
  34.8 4.0 %copy-start.2 = (f32[1,8,256]{2,1,0:T(8,128)S(1)}, f32[1,8,256]{2,1,0:T(8,128)}, u32[]{:S(2)}) copy-start(f32[1,8,256]{2,1,0:T(8,128)} %param.10) | copy-start | bytes 24580
  34.8 4.1 %copy-start.3 = (f32[1,8,256]{2,1,0:T(8,128)S(1)}, f32[1,8,256]{2,1,0:T(8,128)}, u32[]{:S(2)}) copy-start(f32[1,8,256]{2,1,0:T(8,128)} %param.11) | copy-start | bytes 24580
  34.8 16.3 %all-to-all-start.1 = ((f32[32,16,128]{2,1,0:T(8,128)}), f32[32,16,128]{2,1,0:T(8,128)S(1)}, u32[]{:S(2)}, u32[]{:S(2)}) async-start(f32[32,16,128]{2,1,0:T(8,128)} %reorder.1), calls=%async_computation.1 | async-start | bytes 524288 | tf_op jit(solution)/shard_map/all_to_all | solution.py:477
